TPU v7x, 512 devices: a whole 4x8x8 slice. The times are simulated.
512 devices in a mesh: gy: 32 (over z_lo, y, core), gz: 16 (over z_hi, x).
Axes of the slice: x: 4, y: 8, z: 8 (z_hi: 4, z_lo: 2; z = z_hi * 2 + z_lo), core: 2. Of those that a mesh axis runs over, the one named last changes fastest.
Arguments:
- coarse: float32 [8, 1, 1024, 1024], P(None, None, 'gy', 'gz'), may hold values from 0 to 1
- labels: int32 [2, 2048, 2048], P(None, 'gy', 'gz'), may hold values from 0 to 7
- mobility: float32 [8], replicated, may hold values from 0.5 to 2
Outputs:
- phase_field: float32 [8, 2, 2048, 2048], P(None, None, 'gy', 'gz')
All inputs are finite; a program needn't handle non-finite values.
Results may differ from a plain program's by a relative error of at most 0.0001.
Values sent between devices are 32-bit elements; how exact they have to be, the bound alone decides.
No kernel may reach another device: no remote copies, remote signals or barrier semaphores. Data moves between devices by JAX's collectives and lax.ppermute only.
A program may use at most 64 MiB of HBM per device.

v0:
```python
import jax
import jax.numpy as jnp
from jax import lax
from jax.sharding import PartitionSpec as P

ITERS = 2


STEP = 0.075
GAMMA = 0.5
PIN = 1.0


def padded_2(cells, sides, width):
    for axis, dim in sides:
        count = lax.axis_size(axis)
        head = lax.slice_in_dim(cells, 0, width, axis=dim)
        tail = lax.slice_in_dim(cells, cells.shape[dim] - width, cells.shape[dim], axis=dim)
        cells = jnp.concatenate(
            [
                lax.ppermute(tail, axis, [(i, (i + 1) % count) for i in range(count)]),
                cells,
                lax.ppermute(head, axis, [((i + 1) % count, i) for i in range(count)]),
            ],
            axis=dim,
        )
    return cells


def refine(field, axis):
    count = field.shape[axis]
    lower = lax.slice_in_dim(field, 0, count - 1, axis=axis)
    upper = lax.slice_in_dim(field, 1, count, axis=axis)
    odd_cells = 0.75 * lower + 0.25 * upper
    even_cells = 0.75 * upper + 0.25 * lower
    paired = jnp.stack([odd_cells, even_cells], axis=axis + 1)
    shape = list(field.shape)
    shape[axis] = 2 * (count - 1)
    return paired.reshape(shape)


def advance(padded, labels, mobility):
    center = padded[:, :, 1:-1, 1:-1]
    lap = jnp.roll(center, 1, 1) + jnp.roll(center, -1, 1)
    lap = lap + padded[:, :, 2:, 1:-1] + padded[:, :, :-2, 1:-1]
    lap = lap + padded[:, :, 1:-1, 2:] + padded[:, :, 1:-1, :-2] - 6.0 * center
    phases = jnp.arange(center.shape[0], dtype=jnp.int32)
    onehot = (labels[None] == phases[:, None, None, None]).astype(jnp.float32)
    squared = center * center
    squares = jnp.sum(squared, axis=0, keepdims=True)
    drive = (
        center * (1.0 - squared)
        - 2.0 * GAMMA * center * (squares - squared)
        + PIN * (onehot - center)
    )
    return center + STEP * mobility[:, None, None, None] * (lap + drive)


def fine_faces(phase):
    return padded_2(phase, (("gy", 2), ("gz", 3)), 1)


def shards(coarse, labels, mobility):
    width = 1
    padded = padded_2(coarse, (("gy", 2), ("gz", 3)), width)
    padded = jnp.pad(padded, ((0, 0), (1, 1), (0, 0), (0, 0)), mode="wrap")
    fine = refine(refine(refine(padded, 1), 2), 3)[:, 1:-1]
    rim = 2 * width - 1
    phase = fine[:, :, rim:-rim, rim:-rim]
    for step in range(ITERS):
        phase = advance(fine_faces(phase), labels, mobility)
    return phase


def solution(mesh):
    in_specs = (P(None, None, "gy", "gz"), P(None, "gy", "gz"), P())
    out_specs = P(None, None, "gy", "gz")
    return jax.shard_map(shards, mesh=mesh, in_specs=in_specs, out_specs=out_specs, check_vma=False)
```

profile of v0, /device:TPU:57, one launch (start us, length us, event | category | flops | bytes accessed | tf_op | source)
XLA Modules:
  0.0 114.0 jit_solution(5310457744125602556)
XLA Ops:
  0.0 0.8 fusion.34
  0.8 3.8 %collective-permute-start = (f32[8,1,1,64]{3,2,1,0:T(1,128)S(1)}, f32[8,1,1,64]{3,2,1,0:T(1,128)S(1)}, u32[]{:S(2)}, u32[]{:S(2)}) collective-permute-start(f32[8,1,1,64]{3,2,1,0:T(1,128)S(1)} %get-tuple-element.23), channel_id=1, source_target_pairs={{0,16},{16,32},{32,48},{48,64},{64,80},{80,96},{96,112},{112,128},... | collective-permute-start | bytes 6152 | tf_op jit(solution)/shard_map/ppermute | solution.py:21
  4.5 1.9 %collective-permute-start.1 = (f32[8,1,1,64]{3,2,1,0:T(1,128)S(1)}, f32[8,1,1,64]{3,2,1,0:T(1,128)S(1)}, u32[]{:S(2)}, u32[]{:S(2)}) collective-permute-start(f32[8,1,1,64]{3,2,1,0:T(1,128)S(1)} %get-tuple-element.24), channel_id=1, source_target_pairs={{16,0},{32,16},{48,32},{64,48},{80,64},{96,80},{112,96},{128,112},... | collective-permute-start | bytes 6152 | tf_op jit(solution)/shard_map/ppermute | solution.py:23
  6.5 5.1 %collective-permute-done.1 = f32[8,1,1,64]{3,2,1,0:T(1,128)S(1)} collective-permute-done((f32[8,1,1,64]{3,2,1,0:T(1,128)S(1)}, f32[8,1,1,64]{3,2,1,0:T(1,128)S(1)}, u32[]{:S(2)}, u32[]{:S(2)}) %collective-permute-start.1) | collective-permute-done | bytes 2080 | tf_op jit(solution)/shard_map/ppermute | solution.py:23
  11.6 0.9 pad_maximum_fusion.19
  12.5 0.1 fusion.33
  12.6 3.1 %collective-permute-start.2 = (f32[8,1,34,1]{3,2,1,0:T(8,128)S(1)}, f32[8,1,34,1]{3,2,1,0:T(8,128)S(1)}, u32[]{:S(2)}, u32[]{:S(2)}) collective-permute-start(f32[8,1,34,1]{3,2,1,0:T(8,128)S(1)} %get-tuple-element.21), channel_id=1, source_target_pairs={{0,1},{1,2},{2,3},{3,4},{4,5},{5,6},{6,7},{7,8},{8,9},{9,10},{10,1... | collective-permute-start | bytes 3272 | tf_op jit(solution)/shard_map/ppermute | solution.py:21
  15.8 10.8 %collective-permute-start.3 = (f32[8,1,34,1]{3,2,1,0:T(8,128)S(1)}, f32[8,1,34,1]{3,2,1,0:T(8,128)S(1)}, u32[]{:S(2)}, u32[]{:S(2)}) collective-permute-start(f32[8,1,34,1]{3,2,1,0:T(8,128)S(1)} %get-tuple-element.22), channel_id=1, source_target_pairs={{1,0},{2,1},{3,2},{4,3},{5,4},{6,5},{7,6},{8,7},{9,8},{10,9},{11,1... | collective-permute-start | bytes 3272 | tf_op jit(solution)/shard_map/ppermute | solution.py:23
  26.5 0.9 collective-permute-done.2
  27.4 4.8 %collective-permute-done.3 = f32[8,1,34,1]{3,2,1,0:T(8,128)S(1)} collective-permute-done((f32[8,1,34,1]{3,2,1,0:T(8,128)S(1)}, f32[8,1,34,1]{3,2,1,0:T(8,128)S(1)}, u32[]{:S(2)}, u32[]{:S(2)}) %collective-permute-start.3) | collective-permute-done | bytes 1120 | tf_op jit(solution)/shard_map/ppermute | solution.py:23
  32.1 1.1 maximum_bitcast_fusion
  33.3 0.1 add_bitcast_fusion.3
  33.4 0.1 pad_maximum_fusion.1
  33.5 0.3 add_bitcast_fusion.1
  33.8 1.5 %pad_maximum_fusion = f32[8,4,66,65,2]{3,0,2,1,4:T(8,128)} fusion(f32[8,4,66,65,1]{3,0,2,1,4:T(8,128)S(1)} %get-tuple-element.14, f32[8,4,66,65,1]{3,0,2,1,4:T(8,128)S(1)} %get-tuple-element.13), kind=kLoop, calls=%fused_computation.2 | loop fusion | flops 274560 | bytes 2196480 | tf_op jit(solution)/shard_map/stack | solution.py:36
  35.3 2.5 %copy.15 = f32[8,4,66,65,2]{2,0,4,3,1:T(8,128)S(1)} copy(f32[8,4,66,65,2]{3,0,2,1,4:T(8,128)} %pad_maximum_fusion) | data formatting | bytes 2196480 | tf_op jit(solution)/shard_map/stack | solution.py:36
  37.9 1.6 %fusion.30 = (f32[8,2,1,128]{2,0,3,1:T(8,128)}, f32[8,2,1,128]{2,0,3,1:T(8,128)S(1)}) fusion(f32[8,4,66,130]{2,0,3,1:T(8,128)S(1)} %bitcast.13), kind=kLoop, calls=%fused_computation.69 | loop fusion | bytes 32768 | tf_op jit(solution)/shard_map/slice | solution.py:18
  39.5 1.6 %copy.18 = f32[8,2,1,128]{3,0,2,1:T(8,128)S(1)} copy(f32[8,2,1,128]{2,0,3,1:T(8,128)} %get-tuple-element.11) | data formatting | bytes 16384 | tf_op jit(solution)/shard_map/slice | solution.py:18
  41.0 0.4 copy.16
  41.4 1.9 %collective-permute-start.4 = (f32[8,2,1,128]{3,0,2,1:T(8,128)S(1)}, f32[8,2,1,128]{3,0,2,1:T(8,128)S(1)}, u32[]{:S(2)}, u32[]{:S(2)}) collective-permute-start(f32[8,2,1,128]{3,0,2,1:T(8,128)S(1)} %copy.16), channel_id=1, source_target_pairs={{16,0},{32,16},{48,32},{64,48},{80,64},{96,80},{112,96},{128,112},... | collective-permute-start | bytes 24584 | tf_op jit(solution)/shard_map/ppermute | solution.py:23
  43.3 5.8 %collective-permute-start.5 = (f32[8,2,1,128]{3,0,2,1:T(8,128)S(1)}, f32[8,2,1,128]{3,0,2,1:T(8,128)S(1)}, u32[]{:S(2)}, u32[]{:S(2)}) collective-permute-start(f32[8,2,1,128]{3,0,2,1:T(8,128)S(1)} %copy.18), channel_id=1, source_target_pairs={{0,16},{16,32},{32,48},{48,64},{64,80},{80,96},{96,112},{112,128},... | collective-permute-start | bytes 24584 | tf_op jit(solution)/shard_map/ppermute | solution.py:21
  49.1 0.1 copy.22
  49.2 0.3 slice.149
  49.6 0.3 collective-permute-done.5
  49.9 1.3 %copy.19 = f32[8,2,1,128]{2,0,3,1:T(8,128)} copy(f32[8,2,1,128]{3,0,2,1:T(8,128)S(1)} %collective-permute-done.5) | data formatting | bytes 16384 | tf_op jit(solution)/shard_map/ppermute | solution.py:21
  51.2 0.0 collective-permute-done.4
  51.2 1.4 %copy.17 = f32[8,2,1,128]{2,0,3,1:T(8,128)} copy(f32[8,2,1,128]{3,0,2,1:T(8,128)S(1)} %collective-permute-done.4) | data formatting | bytes 16384 | tf_op jit(solution)/shard_map/ppermute | solution.py:23
  52.6 0.9 pad_maximum_fusion.25
  53.5 8.2 %collective-permute-start.6 = (f32[8,2,66,1]{2,0,3,1:T(8,128)S(1)}, f32[8,2,66,1]{2,0,3,1:T(8,128)S(1)}, u32[]{:S(2)}, u32[]{:S(2)}) collective-permute-start(f32[8,2,66,1]{2,0,3,1:T(8,128)S(1)} %get-tuple-element.7), channel_id=1, source_target_pairs={{1,0},{2,1},{3,2},{4,3},{5,4},{6,5},{7,6},{8,7},{9,8},{10,9},{11,1... | collective-permute-start | bytes 12680 | tf_op jit(solution)/shard_map/ppermute | solution.py:23
  61.7 1.9 %collective-permute-start.7 = (f32[8,2,66,1]{2,0,3,1:T(8,128)S(1)}, f32[8,2,66,1]{2,0,3,1:T(8,128)S(1)}, u32[]{:S(2)}, u32[]{:S(2)}) collective-permute-start(f32[8,2,66,1]{2,0,3,1:T(8,128)S(1)} %get-tuple-element.8), channel_id=1, source_target_pairs={{0,1},{1,2},{2,3},{3,4},{4,5},{5,6},{6,7},{7,8},{8,9},{9,10},{10,1... | collective-permute-start | bytes 12680 | tf_op jit(solution)/shard_map/ppermute | solution.py:21
  63.7 0.3 fusion.29
  64.0 6.3 %collective-permute-done.7 = f32[8,2,66,1]{2,0,3,1:T(8,128)S(1)} collective-permute-done((f32[8,2,66,1]{2,0,3,1:T(8,128)S(1)}, f32[8,2,66,1]{2,0,3,1:T(8,128)S(1)}, u32[]{:S(2)}, u32[]{:S(2)}) %collective-permute-start.7) | collective-permute-done | bytes 4256 | tf_op jit(solution)/shard_map/ppermute | solution.py:21
  70.4 10.9 %fusion.22 = f32[8,2,64,128]{2,0,3,1:T(8,128)S(1)} fusion(f32[8,2,64,128]{2,0,3,1:T(8,128)S(1)} %copy-done.1, f32[8,2,66,1]{2,0,3,1:T(8,128)S(1)} %collective-permute-done.7, f32[8,2,1,128]{2,0,3,1:T(8,128)S(1)} %copy-done.3, f32[8,2,1,128]{2,0,3,1:T(8,128)S(1)} %copy-done.2, f32[8,2,66,1]{2,0,3,1:T(8,128)S(1)} %collective-permute-done.6, ...), kind=kOutput, calls=%fused_computation.37 | output fusion | flops 3948551 | bytes 6963712 | tf_op jit(solution)/shard_map/sub | solution.py:53
  81.3 0.3 fusion.32
  81.6 0.4 copy.25
  82.0 7.7 %collective-permute-start.9 = (f32[8,2,1,128]{3,0,2,1:T(8,128)S(1)}, f32[8,2,1,128]{3,0,2,1:T(8,128)S(1)}, u32[]{:S(2)}, u32[]{:S(2)}) collective-permute-start(f32[8,2,1,128]{3,0,2,1:T(8,128)S(1)} %copy.25), channel_id=1, source_target_pairs={{0,16},{16,32},{32,48},{48,64},{64,80},{80,96},{96,112},{112,128},... | collective-permute-start | bytes 24584 | tf_op jit(solution)/shard_map/ppermute | solution.py:21
  89.7 0.4 copy.23
  90.1 1.9 %collective-permute-start.8 = (f32[8,2,1,128]{3,0,2,1:T(8,128)S(1)}, f32[8,2,1,128]{3,0,2,1:T(8,128)S(1)}, u32[]{:S(2)}, u32[]{:S(2)}) collective-permute-start(f32[8,2,1,128]{3,0,2,1:T(8,128)S(1)} %copy.23), channel_id=1, source_target_pairs={{16,0},{32,16},{48,32},{64,48},{80,64},{96,80},{112,96},{128,112},... | collective-permute-start | bytes 24584 | tf_op jit(solution)/shard_map/ppermute | solution.py:23
  92.0 0.4 copy.26
  92.4 4.7 %collective-permute-done.8 = f32[8,2,1,128]{3,0,2,1:T(8,128)S(1)} collective-permute-done((f32[8,2,1,128]{3,0,2,1:T(8,128)S(1)}, f32[8,2,1,128]{3,0,2,1:T(8,128)S(1)}, u32[]{:S(2)}, u32[]{:S(2)}) %collective-permute-start.8) | collective-permute-done | bytes 8224 | tf_op jit(solution)/shard_map/ppermute | solution.py:23
  97.2 0.4 copy.24
  97.6 0.1 pad_maximum_fusion.22
  97.6 1.9 %collective-permute-start.10 = (f32[8,2,66,1]{2,0,3,1:T(8,128)S(1)}, f32[8,2,66,1]{2,0,3,1:T(8,128)S(1)}, u32[]{:S(2)}, u32[]{:S(2)}) collective-permute-start(f32[8,2,66,1]{2,0,3,1:T(8,128)S(1)} %get-tuple-element.5), channel_id=1, source_target_pairs={{1,0},{2,1},{3,2},{4,3},{5,4},{6,5},{7,6},{8,7},{9,8},{10,9},{11,1... | collective-permute-start | bytes 12680 | tf_op jit(solution)/shard_map/ppermute | solution.py:23
  99.6 3.4 %collective-permute-start.11 = (f32[8,2,66,1]{2,0,3,1:T(8,128)S(1)}, f32[8,2,66,1]{2,0,3,1:T(8,128)S(1)}, u32[]{:S(2)}, u32[]{:S(2)}) collective-permute-start(f32[8,2,66,1]{2,0,3,1:T(8,128)S(1)} %get-tuple-element.6), channel_id=1, source_target_pairs={{0,1},{1,2},{2,3},{3,4},{4,5},{5,6},{6,7},{7,8},{8,9},{9,10},{10,1... | collective-permute-start | bytes 12680 | tf_op jit(solution)/shard_map/ppermute | solution.py:21
  102.9 0.1 fusion.31
  103.0 5.2 %collective-permute-done.11 = f32[8,2,66,1]{2,0,3,1:T(8,128)S(1)} collective-permute-done((f32[8,2,66,1]{2,0,3,1:T(8,128)S(1)}, f32[8,2,66,1]{2,0,3,1:T(8,128)S(1)}, u32[]{:S(2)}, u32[]{:S(2)}) %collective-permute-start.11) | collective-permute-done | bytes 4256 | tf_op jit(solution)/shard_map/ppermute | solution.py:21
  108.2 3.4 %fusion.14 = f32[8,2,64,128]{2,0,3,1:T(8,128)} fusion(f32[8,2,64,128]{2,0,3,1:T(8,128)S(1)} %fusion.22, f32[8,2,66,1]{2,0,3,1:T(8,128)S(1)} %collective-permute-done.11, f32[8,2,1,128]{2,0,3,1:T(8,128)S(1)} %copy.24, f32[8,2,1,128]{2,0,3,1:T(8,128)S(1)} %copy.26, f32[8,2,66,1]{2,0,3,1:T(8,128)S(1)} %collective-permute-done.10, ...), kind=kOutput, calls=%fused_computation.21 | output fusion | flops 3948551 | bytes 1663264 | tf_op jit(solution)/shard_map/sub | solution.py:53
  111.6 2.3 %copy.29 = f32[8,2,64,128]{3,2,1,0:T(8,128)} copy(f32[8,2,64,128]{2,0,3,1:T(8,128)} %fusion.14) | data formatting | bytes 1048576 | tf_op jit(solution)/shard_map/add | solution.py:56
  (20 shorter events, 0.1 us)
Async XLA Ops:
  0.8 5.7 %collective-permute-start = (f32[8,1,1,64]{3,2,1,0:T(1,128)S(1)}, f32[8,1,1,64]{3,2,1,0:T(1,128)S(1)}, u32[]{:S(2)}, u32[]{:S(2)}) collective-permute-start(f32[8,1,1,64]{3,2,1,0:T(1,128)S(1)} %get-tuple-element.23), channel_id=1, source_target_pairs={{0,16},{16,32},{32,48},{48,64},{64,80},{80,96},{96,112},{112,128},... | collective-permute-start | bytes 6152 | tf_op jit(solution)/shard_map/ppermute | solution.py:21
  4.5 7.0 %collective-permute-start.1 = (f32[8,1,1,64]{3,2,1,0:T(1,128)S(1)}, f32[8,1,1,64]{3,2,1,0:T(1,128)S(1)}, u32[]{:S(2)}, u32[]{:S(2)}) collective-permute-start(f32[8,1,1,64]{3,2,1,0:T(1,128)S(1)} %get-tuple-element.24), channel_id=1, source_target_pairs={{16,0},{32,16},{48,32},{64,48},{80,64},{96,80},{112,96},{128,112},... | collective-permute-start | bytes 6152 | tf_op jit(solution)/shard_map/ppermute | solution.py:23
  12.6 14.8 %collective-permute-start.2 = (f32[8,1,34,1]{3,2,1,0:T(8,128)S(1)}, f32[8,1,34,1]{3,2,1,0:T(8,128)S(1)}, u32[]{:S(2)}, u32[]{:S(2)}) collective-permute-start(f32[8,1,34,1]{3,2,1,0:T(8,128)S(1)} %get-tuple-element.21), channel_id=1, source_target_pairs={{0,1},{1,2},{2,3},{3,4},{4,5},{5,6},{6,7},{7,8},{8,9},{9,10},{10,1... | collective-permute-start | bytes 3272 | tf_op jit(solution)/shard_map/ppermute | solution.py:21
  15.8 16.4 %collective-permute-start.3 = (f32[8,1,34,1]{3,2,1,0:T(8,128)S(1)}, f32[8,1,34,1]{3,2,1,0:T(8,128)S(1)}, u32[]{:S(2)}, u32[]{:S(2)}) collective-permute-start(f32[8,1,34,1]{3,2,1,0:T(8,128)S(1)} %get-tuple-element.22), channel_id=1, source_target_pairs={{1,0},{2,1},{3,2},{4,3},{5,4},{6,5},{7,6},{8,7},{9,8},{10,9},{11,1... | collective-permute-start | bytes 3272 | tf_op jit(solution)/shard_map/ppermute | solution.py:23
  39.4 9.7 %copy-start.5 = (f32[8]{0:T(128)S(1)}, f32[8]{0:T(128)}, u32[]{:S(2)}) copy-start(f32[8]{0:T(128)} %param.5) | copy-start | bytes 100
  39.5 9.7 %copy-start.4 = (s32[2,64,128]{2,1,0:T(8,128)S(1)}, s32[2,64,128]{2,1,0:T(8,128)}, u32[]{:S(2)}) copy-start(s32[2,64,128]{2,1,0:T(8,128)} %param.4) | copy-start | bytes 196612
  41.4 9.8 %collective-permute-start.4 = (f32[8,2,1,128]{3,0,2,1:T(8,128)S(1)}, f32[8,2,1,128]{3,0,2,1:T(8,128)S(1)}, u32[]{:S(2)}, u32[]{:S(2)}) collective-permute-start(f32[8,2,1,128]{3,0,2,1:T(8,128)S(1)} %copy.16), channel_id=1, source_target_pairs={{16,0},{32,16},{48,32},{64,48},{80,64},{96,80},{112,96},{128,112},... | collective-permute-start | bytes 24584 | tf_op jit(solution)/shard_map/ppermute | solution.py:23
  43.3 6.5 %collective-permute-start.5 = (f32[8,2,1,128]{3,0,2,1:T(8,128)S(1)}, f32[8,2,1,128]{3,0,2,1:T(8,128)S(1)}, u32[]{:S(2)}, u32[]{:S(2)}) collective-permute-start(f32[8,2,1,128]{3,0,2,1:T(8,128)S(1)} %copy.18), channel_id=1, source_target_pairs={{0,16},{16,32},{32,48},{48,64},{64,80},{80,96},{96,112},{112,128},... | collective-permute-start | bytes 24584 | tf_op jit(solution)/shard_map/ppermute | solution.py:21
  49.6 3.9 %copy-start = (f32[8,2,64,128]{2,0,3,1:T(8,128)}, f32[8,2,64,128]{2,0,3,1:T(8,128)S(1)}, u32[]{:S(2)}) copy-start(f32[8,2,64,128]{2,0,3,1:T(8,128)S(1)} %slice.149) | copy-start | bytes 1572868
  52.6 17.8 %copy-start.3 = (f32[8,2,1,128]{2,0,3,1:T(8,128)S(1)}, f32[8,2,1,128]{2,0,3,1:T(8,128)}, u32[]{:S(2)}) copy-start(f32[8,2,1,128]{2,0,3,1:T(8,128)} %copy.17) | copy-start | bytes 24580
  53.5 16.9 %copy-start.2 = (f32[8,2,1,128]{2,0,3,1:T(8,128)S(1)}, f32[8,2,1,128]{2,0,3,1:T(8,128)}, u32[]{:S(2)}) copy-start(f32[8,2,1,128]{2,0,3,1:T(8,128)} %copy.19) | copy-start | bytes 24580
  53.5 16.8 %copy-start.1 = (f32[8,2,64,128]{2,0,3,1:T(8,128)S(1)}, f32[8,2,64,128]{2,0,3,1:T(8,128)}, u32[]{:S(2)}) copy-start(f32[8,2,64,128]{2,0,3,1:T(8,128)} %copy-done) | copy-start | bytes 1572868
  53.5 10.5 %collective-permute-start.6 = (f32[8,2,66,1]{2,0,3,1:T(8,128)S(1)}, f32[8,2,66,1]{2,0,3,1:T(8,128)S(1)}, u32[]{:S(2)}, u32[]{:S(2)}) collective-permute-start(f32[8,2,66,1]{2,0,3,1:T(8,128)S(1)} %get-tuple-element.7), channel_id=1, source_target_pairs={{1,0},{2,1},{3,2},{4,3},{5,4},{6,5},{7,6},{8,7},{9,8},{10,9},{11,1... | collective-permute-start | bytes 12680 | tf_op jit(solution)/shard_map/ppermute | solution.py:23
  61.7 8.6 %collective-permute-start.7 = (f32[8,2,66,1]{2,0,3,1:T(8,128)S(1)}, f32[8,2,66,1]{2,0,3,1:T(8,128)S(1)}, u32[]{:S(2)}, u32[]{:S(2)}) collective-permute-start(f32[8,2,66,1]{2,0,3,1:T(8,128)S(1)} %get-tuple-element.8), channel_id=1, source_target_pairs={{0,1},{1,2},{2,3},{3,4},{4,5},{5,6},{6,7},{7,8},{8,9},{9,10},{10,1... | collective-permute-start | bytes 12680 | tf_op jit(solution)/shard_map/ppermute | solution.py:21
  82.0 10.0 %collective-permute-start.9 = (f32[8,2,1,128]{3,0,2,1:T(8,128)S(1)}, f32[8,2,1,128]{3,0,2,1:T(8,128)S(1)}, u32[]{:S(2)}, u32[]{:S(2)}) collective-permute-start(f32[8,2,1,128]{3,0,2,1:T(8,128)S(1)} %copy.25), channel_id=1, source_target_pairs={{0,16},{16,32},{32,48},{48,64},{64,80},{80,96},{96,112},{112,128},... | collective-permute-start | bytes 24584 | tf_op jit(solution)/shard_map/ppermute | solution.py:21
  90.1 7.1 %collective-permute-start.8 = (f32[8,2,1,128]{3,0,2,1:T(8,128)S(1)}, f32[8,2,1,128]{3,0,2,1:T(8,128)S(1)}, u32[]{:S(2)}, u32[]{:S(2)}) collective-permute-start(f32[8,2,1,128]{3,0,2,1:T(8,128)S(1)} %copy.23), channel_id=1, source_target_pairs={{16,0},{32,16},{48,32},{64,48},{80,64},{96,80},{112,96},{128,112},... | collective-permute-start | bytes 24584 | tf_op jit(solution)/shard_map/ppermute | solution.py:23
  97.6 5.4 %collective-permute-start.10 = (f32[8,2,66,1]{2,0,3,1:T(8,128)S(1)}, f32[8,2,66,1]{2,0,3,1:T(8,128)S(1)}, u32[]{:S(2)}, u32[]{:S(2)}) collective-permute-start(f32[8,2,66,1]{2,0,3,1:T(8,128)S(1)} %get-tuple-element.5), channel_id=1, source_target_pairs={{1,0},{2,1},{3,2},{4,3},{5,4},{6,5},{7,6},{8,7},{9,8},{10,9},{11,1... | collective-permute-start | bytes 12680 | tf_op jit(solution)/shard_map/ppermute | solution.py:23
  99.6 8.6 %collective-permute-start.11 = (f32[8,2,66,1]{2,0,3,1:T(8,128)S(1)}, f32[8,2,66,1]{2,0,3,1:T(8,128)S(1)}, u32[]{:S(2)}, u32[]{:S(2)}) collective-permute-start(f32[8,2,66,1]{2,0,3,1:T(8,128)S(1)} %get-tuple-element.6), channel_id=1, source_target_pairs={{0,1},{1,2},{2,3},{3,4},{4,5},{5,6},{6,7},{7,8},{8,9},{9,10},{10,1... | collective-permute-start | bytes 12680 | tf_op jit(solution)/shard_map/ppermute | solution.py:21
where the time goes:
time: 115 us; the launch traced here: 114 us
  starting transfers between devices  52.3 us (45%)
  waiting for transfers between devices  27.2 us (24%)
  other arithmetic  19.4 us (17%)
  local copies, waits for them, and re-layouts  14.7 us (13%)
    ppermute x6, starting transfers between devices, padded_2(): lax.ppermute(head, axis, [((i + 1) % count, i) for i in range(count)])  26.7 us
    ppermute x6, starting transfers between devices, padded_2(): lax.ppermute(tail, axis, [(i, (i + 1) % count) for i in range(count)])  25.6 us
    ppermute x6, waiting for transfers between devices, padded_2(): lax.ppermute(head, axis, [((i + 1) % count, i) for i in range(count)])  14.6 us
    sub x2, other arithmetic, advance(): squares - squared  14.3 us
    ppermute x6, waiting for transfers between devices, padded_2(): lax.ppermute(tail, axis, [(i, (i + 1) % count) for i in range(count)])  12.7 us
    slice x6, local copies, waits for them, and re-layouts, padded_2(): lax.slice_in_dim(cells, cells.shape[dim] - width, cells.shape[dim], axis=...  4.75 us
    another operation x1, local copies, waits for them, and re-layouts, refine(): paired = jnp.stack([odd_cells, even_cells], axis=axis + 1)  2.51 us
    add x1, local copies, waits for them, and re-layouts, advance(): return center + STEP * mobility[:, None, None, None] * (lap + drive)  2.34 us
  transfers between devices with their start and end apart: 12, of which 7 were waited for; matrix products, arithmetic and copies ran while one was open for 3% of the time, Pallas kernels for 0%

commit v1 on v0

v1 whole, which is shorter than its diff:
```python
import jax
import jax.numpy as jnp
from jax import lax
from jax.experimental import pallas as pl
from jax.experimental.pallas import tpu as pltpu
from jax.sharding import PartitionSpec as P

STEP = 0.075
NP = 8
CR, CC = 32, 64
FR, FC = 64, 128
YROWS = 48
ZROWS = 48
F32 = jnp.float32


def lanes(rows):
    return lax.broadcasted_iota(jnp.int32, (rows, 128), 1)


def pack_kernel(coarse, labels, strip, cols):
    lane = lanes(CR)
    packed = jnp.zeros((CR, 128), F32)
    for p in range(NP):
        own = coarse[p]
        both = jnp.concatenate([own, own], axis=1)
        packed = jnp.where(lane // 4 == p, pltpu.roll(both, (4 * p - 62) % 128, 1), packed)
        strip[4 * p : 4 * p + 2, :] = both[30:32]
        strip[4 * p + 2 : 4 * p + 4, :] = both[0:2]
    for x in range(2):
        marks = labels[x].astype(F32)
        spot = 32 + 4 * x
        packed = jnp.where(lane // 2 == spot // 2, pltpu.roll(marks[:CR], spot + 1, 1), packed)
        packed = jnp.where(lane // 2 == spot // 2 + 1, pltpu.roll(marks[CR:], spot + 3, 1), packed)
        strip[32 + 2 * x : 33 + 2 * x, :] = marks[FR - 1 : FR]
        strip[33 + 2 * x : 34 + 2 * x, :] = marks[0:1]
    cols[...] = packed
    strip[36:40, :] = jnp.zeros((4, 128), F32)
    strip[40:42, :] = packed[30:32]
    strip[42:44, :] = packed[0:2]
    strip[44:48, :] = jnp.zeros((4, 128), F32)


def z_weights():
    k = lax.broadcasted_iota(jnp.int32, (256, 256), 0) % 128
    n = lax.broadcasted_iota(jnp.int32, (256, 256), 1)
    z = jnp.where(n < 128, n, jnp.where(n == 128, -1, jnp.where(n == 255, 128, jnp.where(n == 254, -2, jnp.where(n == 253, 129, 999)))))
    column = jnp.where(k < 64, k, jnp.where(k < 66, k - 66, jnp.where(k < 68, k - 2, -999)))
    near = z >> 1
    far = near + 2 * (z & 1) - 1
    return (0.75 * (column == near).astype(F32) + 0.25 * (column == far).astype(F32)).astype(jnp.bfloat16)


def relax_kernel(mobility, coarse, labels, ya, yb, za, zb, out, pad, zm, ze, fm, fe, lm, le, pm, pe):
    y_even = lax.axis_index("gy") % 2 == 0
    z_even = lax.axis_index("gz") % 2 == 0
    high = jnp.where(y_even, ya[1], yb[...])
    low = jnp.where(y_even, yb[...], ya[0])
    left = jnp.where(z_even, zb[0], za[...])
    right = jnp.where(z_even, za[...], zb[1])

    lane = lanes(ZROWS)
    halo = jnp.where(lane % 4 < 2, left, right)
    corner_high = jnp.where(y_even, halo[36:40], halo[40:44])
    corner_low = jnp.where(y_even, halo[40:44], halo[32:36])
    for p in range(NP):
        turn = (64 - 4 * p) % 128
        pad[p, 8 : 8 + CR, :] = pltpu.roll(halo[:CR], turn, 1)
        pad[p, 8 : 8 + CR, 0:CC] = coarse[p]
        inner = lane[0:2] < CC
        pad[p, 6:8, :] = jnp.where(inner, low[4 * p : 4 * p + 2], pltpu.roll(corner_low, turn, 1)[0:2])
        pad[p, 40:42, :] = jnp.where(inner, high[4 * p + 2 : 4 * p + 4], pltpu.roll(corner_high, turn, 1)[2:4])

    cells = pad[...].reshape(NP * 48, 128)
    first = cells.astype(jnp.bfloat16)
    second = (cells - first.astype(F32)).astype(jnp.bfloat16)
    fine = jnp.dot(jnp.concatenate([first, second], axis=1), z_weights(), preferred_element_type=F32)
    zm[...] = fine[:, :128].reshape(NP, 48, 128)
    ze[...] = fine[:, 128:].reshape(NP, 48, 128)
    for p in range(NP):
        for src, dst in ((zm, fm), (ze, fe)):
            mid = 0.75 * src[p, 7:41, :]
            dst[p, pl.ds(6, 34, stride=2), :] = mid + 0.25 * src[p, 6:40, :]
            dst[p, pl.ds(7, 34, stride=2), :] = mid + 0.25 * src[p, 8:42, :]

    marks = jnp.where(lane[:CR] % 2 == 0, pltpu.roll(right[:CR], 127, 1), pltpu.roll(left[:CR], 1, 1))
    for x in range(2):
        lm[x, 8 : 8 + FR, :] = labels[x].astype(F32)
        lm[x, 7:8, :] = low[32 + 2 * x : 33 + 2 * x]
        lm[x, 72:73, :] = high[33 + 2 * x : 34 + 2 * x]
        le[x, 8 : 8 + CR, :] = pltpu.roll(marks, 95 - 4 * x, 1)
        le[x, 8 + CR : 8 + FR, :] = pltpu.roll(marks, 93 - 4 * x, 1)

    rate = [STEP * mobility[p] for p in range(NP)]
    lane8 = lanes(8)
    first_lane, last_lane = lane8 == 0, lane8 == 127

    for t in range(9):
        here = pl.ds(7 + 8 * t, 8)
        above, below = pl.ds(6 + 8 * t, 8), pl.ds(8 + 8 * t, 8)
        ms = [fm[p, here, :] for p in range(NP)]
        es = [fe[p, here, :] for p in range(NP)]
        sm = 4.0 + sum(m * m for m in ms)
        se = 4.0 + sum(e * e for e in es)
        marks_m = [lm[x, here, :] for x in range(2)]
        marks_e = [le[x, here, :] for x in range(2)]
        for p in range(NP):
            m, e = ms[p], es[p]
            west = jnp.where(first_lane, e, pltpu.roll(m, 1, 1))
            east = jnp.where(last_lane, e, pltpu.roll(m, 127, 1))
            lap = (fm[p, above, :] + fm[p, below, :]) + (west + east)
            base = m + rate[p] * (lap - sm * m)
            lap_e = (fe[p, above, :] + fe[p, below, :]) + (m + pltpu.roll(e, 2, 1))
            base_e = e + rate[p] * (lap_e - se * e)
            for x in range(2):
                pm[x, p, here, :] = jnp.where(marks_m[x] == p, base + rate[p], base)
                pe[x, p, here, :] = jnp.where(marks_e[x] == p, base_e + rate[p], base_e)

    for t in range(8):
        here = pl.ds(8 + 8 * t, 8)
        above, below = pl.ds(7 + 8 * t, 8), pl.ds(9 + 8 * t, 8)
        for x in range(2):
            ms = [pm[x, p, here, :] for p in range(NP)]
            sm = 6.0 + sum(m * m for m in ms)
            marks_m = lm[x, here, :]
            for p in range(NP):
                m, e, other = ms[p], pe[x, p, here, :], pm[1 - x, p, here, :]
                west = jnp.where(first_lane, e, pltpu.roll(m, 1, 1))
                east = jnp.where(last_lane, e, pltpu.roll(m, 127, 1))
                lap = (pm[x, p, above, :] + pm[x, p, below, :]) + (west + east) + (other + other)
                change = lap - sm * m
                change = jnp.where(marks_m == p, change + 1.0, change)
                out[p, x, 8 * t : 8 * t + 8, :] = m + rate[p] * change


def swapped(cells, axis, odd):
    count = lax.axis_size(axis)
    pairs = []
    for i in range(odd, count, 2):
        j = (i + 1) % count
        pairs += [(i, j), (j, i)]
    return lax.ppermute(cells, axis, pairs)


def paired(cells, axis, odd):
    count = lax.axis_size(axis)
    return lax.all_gather(cells, axis, axis_index_groups=[[i, (i + 1) % count] for i in range(odd, count, 2)])


def shards(coarse, labels, mobility):
    coarse = coarse.reshape(NP, CR, CC)
    vmem = pl.BlockSpec(memory_space=pltpu.VMEM)
    strip, cols = pl.pallas_call(
        pack_kernel,
        out_shape=(jax.ShapeDtypeStruct((YROWS, 128), F32), jax.ShapeDtypeStruct((CR, 128), F32)),
        in_specs=[vmem, vmem],
        out_specs=(vmem, vmem),
        compiler_params=pltpu.CompilerParams(vmem_limit_bytes=8 << 20),
        cost_estimate=pl.CostEstimate(flops=20000, bytes_accessed=200000, transcendentals=0),
        name="pack",
    )(coarse, labels)
    yb = swapped(strip, "gy", 1)
    ya = paired(strip, "gy", 0)
    sides = jnp.concatenate([cols, ya[0, 40:44], ya[1, 40:44], yb[40:44], jnp.zeros((4, 128), F32)])
    za = swapped(sides, "gz", 0)
    zb = paired(sides, "gz", 1)
    tile = lambda *shape: pltpu.VMEM(shape + (128,), F32)
    out = pl.pallas_call(
        relax_kernel,
        out_shape=jax.ShapeDtypeStruct((NP, 2, FR, FC), F32),
        in_specs=[pl.BlockSpec(memory_space=pltpu.SMEM)] + [vmem] * 6,
        out_specs=vmem,
        scratch_shapes=[
            tile(NP, 48),
            tile(NP, 48),
            tile(NP, 48),
            tile(NP, 88),
            tile(NP, 88),
            tile(2, 80),
            tile(2, 80),
            tile(2, NP, 80),
            tile(2, NP, 80),
        ],
        compiler_params=pltpu.CompilerParams(vmem_limit_bytes=16 << 20),
        cost_estimate=pl.CostEstimate(flops=8000000, bytes_accessed=900000, transcendentals=0),
        name="relax",
    )(mobility, coarse, labels, ya, yb, za, zb)
    return out


def solution(mesh):
    in_specs = (P(None, None, "gy", "gz"), P(None, "gy", "gz"), P())
    out_specs = P(None, None, "gy", "gz")
    return jax.shard_map(shards, mesh=mesh, in_specs=in_specs, out_specs=out_specs, check_vma=False)
```

time: 115 us -> 29.3 us (0.25)
  the two profiles are of different devices: /device:TPU:57 before, /device:TPU:1 now
where the time goes in v1:
time: 29.3 us; the launch traced here: 29.1 us
  blocking collectives  16.9 us (58%)
  starting transfers between devices  7.17 us (24%)
  Pallas kernels  2.46 us (8%)
  local copies, waits for them, and re-layouts  2.44 us (8%)
    all_gather x2, blocking collectives, paired(): lax.all_gather(cells, axis, axis_index_groups=[[i, (i + 1) % count] for i...  16.9 us
    ppermute x2, starting transfers between devices, swapped(): return lax.ppermute(cells, axis, pairs)  7.17 us
    unnamed x10, local copies, waits for them, and re-layouts  2.39 us
    pallas_call x1, Pallas kernels, shards(): pl.pallas_call(relax_kernel, out_shape=jax.ShapeDtypeStruct((NP, 2, FR, F...  2.29 us
  transfers between devices with their start and end apart: 2, of which 0 were waited for; matrix products, arithmetic and copies ran while one was open for 0% of the time, Pallas kernels for 0%

profile of v1, /device:TPU:1, one launch (start us, length us, event | category | flops | bytes accessed | tf_op | source)
XLA Modules:
  0.0 29.1 jit_solution(12178095845627010738)
XLA Ops:
  0.0 0.0 copy-start
  0.0 0.9 %copy-done = f32[8,1,32,64]{3,2,1,0:T(8,128)S(1)} copy-done((f32[8,1,32,64]{3,2,1,0:T(8,128)S(1)}, f32[8,1,32,64]{3,2,1,0:T(8,128)}, u32[]{:S(2)}) %copy-start) | copy-done | bytes 65560
  0.9 0.0 copy-start.2
  0.9 0.8 %copy-done.2 = s32[2,64,128]{2,1,0:T(8,128)S(1)} copy-done((s32[2,64,128]{2,1,0:T(8,128)S(1)}, s32[2,64,128]{2,1,0:T(8,128)}, u32[]{:S(2)}) %copy-start.2) | copy-done | bytes 65560
  1.7 0.2 pack.1
  1.9 0.0 copy-start.1
  1.9 4.7 %collective-permute-start = (f32[48,128]{1,0:T(8,128)S(1)}, f32[48,128]{1,0:T(8,128)S(1)}, u32[]{:S(2)}, u32[]{:S(2)}) collective-permute-start(f32[48,128]{1,0:T(8,128)S(1)} %get-tuple-element.7), channel_id=1, source_target_pairs={{16,32},{32,16},{48,64},{64,48},{80,96},{96,80},{112,128},{128,112... | collective-permute-start | bytes 73736 | tf_op jit(solution)/shard_map/ppermute | solution.py:142
  6.7 5.7 %all-gather = f32[96,128]{1,0:T(8,128)S(1)} all-gather(f32[48,128]{1,0:T(8,128)S(1)} %get-tuple-element.7), channel_id=2, replica_groups={{0,16},{32,48},{64,80},{96,112},{128,144},{160,176},{192,208},{224,240}..., dimensions={0}, use_global_device_ids=true | all-gather | bytes 73728 | tf_op jit(solution)/shard_map/all_gather | solution.py:147
  12.4 0.0 collective-permute-done.yb
  12.4 0.0 copy-start.3
  12.4 2.4 %collective-permute-start.1 = (f32[48,128]{1,0:T(8,128)S(1)}, f32[48,128]{1,0:T(8,128)S(1)}, u32[]{:S(2)}, u32[]{:S(2)}) collective-permute-start(f32[48,128]{1,0:T(8,128)S(1)} %concatenate.3), channel_id=1, source_target_pairs={{0,1},{1,0},{2,3},{3,2},{4,5},{5,4},{6,7},{7,6},{8,9},{9,8},{10,11... | collective-permute-start | bytes 73736 | tf_op jit(solution)/shard_map/ppermute | solution.py:142
  14.9 11.2 %all-gather.1 = f32[96,128]{1,0:T(8,128)S(1)} all-gather(f32[48,128]{1,0:T(8,128)S(1)} %concatenate.3), channel_id=3, replica_groups={{1,2},{3,4},{5,6},{7,8},{9,10},{11,12},{13,14},{15,0},{17,18},{19,20},{..., dimensions={0}, use_global_device_ids=true | all-gather | bytes 73728 | tf_op jit(solution)/shard_map/all_gather | solution.py:147
  26.1 0.0 copy-start.4
  26.1 0.0 collective-permute-done.1.za
  26.1 0.0 copy-done.1
  26.1 0.0 copy-done.3
  26.2 0.6 %copy-done.4 = f32[8]{0:T(128)S(1)} copy-done((f32[8]{0:T(128)S(1)}, f32[8]{0:T(128)}, u32[]{:S(2)}) %copy-start.4) | copy-done | bytes 56
  26.8 2.3 %relax.1 = f32[8,2,64,128]{3,2,1,0:T(8,128)} custom-call(f32[8]{0:T(128)S(1)} %copy-done.4, f32[8,32,64]{2,1,0:T(8,128)S(1)} %bitcast.8, s32[2,64,128]{2,1,0:T(8,128)S(1)} %copy-done.3, f32[2,48,128]{2,1,0:T(8,128)S(1)} %bitcast.10, f32[48,128]{1,0:T(8,128)S(1)} %collective-permute-done.yb, f32[48,128]{1,0:T(8,128)S(1)} %collective-permute-done.1.za, ...), custom_call_target="tpu_custom_call" | custom-call | flops 8000000 | bytes 900000 | tf_op jit(solution)/shard_map/relax/pallas_call | solution.py:168
  (4 shorter events, 0.1 us)
Async XLA Ops:
  0.0 0.9 %copy-start = (f32[8,1,32,64]{3,2,1,0:T(8,128)S(1)}, f32[8,1,32,64]{3,2,1,0:T(8,128)}, u32[]{:S(2)}) copy-start(f32[8,1,32,64]{3,2,1,0:T(8,128)} %param.3) | copy-start | bytes 196612
  0.9 0.8 %copy-start.2 = (s32[2,64,128]{2,1,0:T(8,128)S(1)}, s32[2,64,128]{2,1,0:T(8,128)}, u32[]{:S(2)}) copy-start(s32[2,64,128]{2,1,0:T(8,128)} %labels.3) | copy-start | bytes 196612
  1.9 24.2 %copy-start.1 = (f32[8,1,32,64]{3,2,1,0:T(8,128)S(1)}, f32[8,1,32,64]{3,2,1,0:T(8,128)}, u32[]{:S(2)}) copy-start(f32[8,1,32,64]{3,2,1,0:T(8,128)} %param.3) | copy-start | bytes 196612
  1.9 10.4 %collective-permute-start = (f32[48,128]{1,0:T(8,128)S(1)}, f32[48,128]{1,0:T(8,128)S(1)}, u32[]{:S(2)}, u32[]{:S(2)}) collective-permute-start(f32[48,128]{1,0:T(8,128)S(1)} %get-tuple-element.7), channel_id=1, source_target_pairs={{16,32},{32,16},{48,64},{64,48},{80,96},{96,80},{112,128},{128,112... | collective-permute-start | bytes 73736 | tf_op jit(solution)/shard_map/ppermute | solution.py:142
  12.4 13.8 %copy-start.3 = (s32[2,64,128]{2,1,0:T(8,128)S(1)}, s32[2,64,128]{2,1,0:T(8,128)}, u32[]{:S(2)}) copy-start(s32[2,64,128]{2,1,0:T(8,128)} %labels.3) | copy-start | bytes 196612
  12.4 13.7 %collective-permute-start.1 = (f32[48,128]{1,0:T(8,128)S(1)}, f32[48,128]{1,0:T(8,128)S(1)}, u32[]{:S(2)}, u32[]{:S(2)}) collective-permute-start(f32[48,128]{1,0:T(8,128)S(1)} %concatenate.3), channel_id=1, source_target_pairs={{0,1},{1,0},{2,3},{3,2},{4,5},{5,4},{6,7},{7,6},{8,9},{9,8},{10,11... | collective-permute-start | bytes 73736 | tf_op jit(solution)/shard_map/ppermute | solution.py:142
  26.1 0.7 %copy-start.4 = (f32[8]{0:T(128)S(1)}, f32[8]{0:T(128)}, u32[]{:S(2)}) copy-start(f32[8]{0:T(128)} %mobility.1) | copy-start | bytes 100

commit v2 on v1

v2 whole, which is shorter than its diff:
```python
import jax
import jax.numpy as jnp
from jax import lax
from jax.experimental import pallas as pl
from jax.experimental.pallas import tpu as pltpu
from jax.sharding import PartitionSpec as P

STEP = 0.075
NP = 8
CR, CC = 32, 64
FR, FC = 64, 128
MROWS = 16
F32 = jnp.float32


def lanes(rows):
    return lax.broadcasted_iota(jnp.int32, (rows, 128), 1)


def parities():
    return lax.axis_index("gy") % 2 == 0, lax.axis_index("gz") % 2 == 0


def strips_kernel(coarse_hbm, labels_hbm, mobility_hbm, to_a, to_b, rates, top, bottom, marks, mobility, low, high, sems):
    copies = [
        pltpu.make_async_copy(src, dst, sems.at[i])
        for i, (src, dst) in enumerate(
            (
                (coarse_hbm.at[:, 0:8, :], top),
                (coarse_hbm.at[:, CR - 8 : CR, :], bottom),
                (labels_hbm.at[:, 0:8, :], marks.at[:, 0:8, :]),
                (labels_hbm.at[:, FR - 8 : FR, :], marks.at[:, 8:16, :]),
                (mobility_hbm, mobility),
            )
        )
    ]
    for copy in copies:
        copy.start()
    y_even, _ = parities()
    for copy in copies:
        copy.wait()
    for row, block, strip in ((0, top, low), (6, bottom, high)):
        for p in range(NP):
            strip[p : p + 1, 0:CC] = block[p, row : row + 1, :]
            strip[p : p + 1, CC : 2 * CC] = block[p, row + 1 : row + 2, :]
        for x in range(2):
            strip[8 + x : 9 + x, :] = marks[x, 15 * (row // 6) : 15 * (row // 6) + 1, :].astype(F32)
        strip[10:16, :] = jnp.zeros((6, 128), F32)
    to_a[...] = jnp.where(y_even, high[...], low[...])
    to_b[...] = jnp.where(y_even, low[...], high[...])
    for p in range(NP):
        rates[p : p + 1, :] = jnp.full((1, 128), STEP * mobility[p], F32)


def columns_kernel(coarse, labels, sides):
    lane = lanes(8)
    first, last = jnp.zeros((8, 128), F32), jnp.zeros((8, 128), F32)
    for g in range(4):
        start = 64 * (g // 2) + 2 * (g % 2)
        for p in range(NP):
            own = jnp.concatenate([coarse[p, 8 * g : 8 * g + 8, :], jnp.zeros((8, CC), F32)], axis=1)
            at = start + 4 * p
            first = jnp.where(lane // 2 == at // 2, pltpu.roll(own, at, 1), first)
            last = jnp.where(lane // 2 == at // 2, pltpu.roll(own, (at - 62) % 128, 1), last)
        for k in range(4):
            at = start + 32 + 4 * k
            cells = labels[k % 2, 32 * (k // 2) + 8 * g : 32 * (k // 2) + 8 * g + 8, :].astype(F32)
            first = jnp.where(lane == at, pltpu.roll(cells, at, 1), first)
            last = jnp.where(lane == at, pltpu.roll(cells, at + 1, 1), last)
    sides[0:8, :] = first
    sides[8:16, :] = last


def picked(ya0, ya1, yb):
    y_even, _ = parities()
    return jnp.where(y_even, yb, ya0), jnp.where(y_even, ya1, yb)


def sides_kernel(columns, ya, yb, sides):
    sides[0:16, :] = columns[...]
    lane = lanes(8)
    ends = jnp.zeros((8, 128), F32)
    for j, strip in enumerate(picked(ya[0, 0:8], ya[1, 0:8], yb[0:8])):
        for i in range(2):
            at = 64 + 16 * j + 8 * i
            ends = jnp.where(lane // 2 == at // 2, pltpu.roll(strip, (at - 62 - 64 * i) % 128, 1), ends)
            ends = jnp.where(lane // 2 == at // 2 + 1, pltpu.roll(strip, (at + 2 - 64 * i) % 128, 1), ends)
    sides[16:24, :] = ends


def z_weights():
    k = lax.broadcasted_iota(jnp.int32, (256, 256), 0) % 128
    n = lax.broadcasted_iota(jnp.int32, (256, 256), 1)
    z = jnp.where(n < 128, n, jnp.where(n == 128, -1, jnp.where(n == 255, 128, jnp.where(n == 254, -2, jnp.where(n == 253, 129, 999)))))
    column = jnp.where(k < 64, k, jnp.where(k < 66, k - 66, jnp.where(k < 68, k - 2, -999)))
    near = z >> 1
    far = near + 2 * (z & 1) - 1
    return (0.75 * (column == near).astype(F32) + 0.25 * (column == far).astype(F32)).astype(jnp.bfloat16)


def relax_kernel(rates, coarse, labels, ya, yb, za0, za1, zb, out_hbm, pad, zm, ze, fm, fe, lm, le, pm, pe, out, sems):
    _, z_even = parities()
    low, high = picked(ya[0], ya[1], yb[...])
    za = za0[...] + za1[...]
    left = jnp.where(z_even, zb[0], za)
    right = jnp.where(z_even, za, zb[1])

    lane8 = lanes(8)
    first_lane, last_lane = lane8 == 0, lane8 == 127
    west, east = left[8:16], right[0:8]
    for g in range(4):
        start = 64 * (g // 2) + 2 * (g % 2)
        for p in range(NP):
            at = start + 4 * p
            beside = jnp.where(lane8 < 66, pltpu.roll(west, (64 - at) % 128, 1), pltpu.roll(east, (66 - at) % 128, 1))
            pad[48 * p + 8 + 8 * g : 48 * p + 16 + 8 * g, :] = beside
        for k in range(4):
            rows = slice(8 + 32 * (k // 2) + 8 * g, 16 + 32 * (k // 2) + 8 * g)
            at = start + 32 + 4 * k
            le[k % 2, rows, :] = jnp.where(first_lane, pltpu.roll(west, 128 - at, 1), pltpu.roll(east, 127 - at, 1))
    for p in range(NP):
        pad[48 * p + 8 : 48 * p + 8 + CR, 0:CC] = coarse[p]
    ends = jnp.where(lane8 % 4 < 2, left[16:24], right[16:24])
    for j, strip in enumerate((low, high)):
        for i in range(2):
            beside = pltpu.roll(ends, (-16 * j - 8 * i) % 128, 1)
            cells = pltpu.roll(strip[0:8], CC, 1) if i else strip[0:8]
            pad[pl.ds(6 + 34 * j + i, NP, stride=48), :] = jnp.where(lane8 < CC, cells, beside)

    cells = pad[...]
    first = cells.astype(jnp.bfloat16)
    second = (cells - first.astype(F32)).astype(jnp.bfloat16)
    fine = jnp.dot(jnp.concatenate([first, second], axis=1), z_weights(), preferred_element_type=F32)
    zm[...] = fine[:, :128].reshape(NP, 48, 128)
    ze[...] = fine[:, 128:].reshape(NP, 48, 128)
    for p in range(NP):
        for src, dst in ((zm, fm), (ze, fe)):
            mid = 0.75 * src[p, 7:41, :]
            dst[p, pl.ds(6, 34, stride=2), :] = mid + 0.25 * src[p, 6:40, :]
            dst[p, pl.ds(7, 34, stride=2), :] = mid + 0.25 * src[p, 8:42, :]

    for x in range(2):
        lm[x, 8 : 8 + FR, :] = labels[x].astype(F32)
        lm[x, 7:8, :] = low[8 + x : 9 + x]
        lm[x, 72:73, :] = high[8 + x : 9 + x]

    rate = [rates[p : p + 1, :] for p in range(NP)]

    for t in range(9):
        here = pl.ds(7 + 8 * t, 8)
        above, below = pl.ds(6 + 8 * t, 8), pl.ds(8 + 8 * t, 8)
        ms = [fm[p, here, :] for p in range(NP)]
        es = [fe[p, here, :] for p in range(NP)]
        sm = 4.0 + sum(m * m for m in ms)
        se = 4.0 + sum(e * e for e in es)
        marks_m = [lm[x, here, :] for x in range(2)]
        marks_e = [le[x, here, :] for x in range(2)]
        for p in range(NP):
            m, e = ms[p], es[p]
            west = jnp.where(first_lane, e, pltpu.roll(m, 1, 1))
            east = jnp.where(last_lane, e, pltpu.roll(m, 127, 1))
            lap = (fm[p, above, :] + fm[p, below, :]) + (west + east)
            base = m + rate[p] * (lap - sm * m)
            lap_e = (fe[p, above, :] + fe[p, below, :]) + (m + pltpu.roll(e, 2, 1))
            base_e = e + rate[p] * (lap_e - se * e)
            for x in range(2):
                pm[x, p, here, :] = jnp.where(marks_m[x] == p, base + rate[p], base)
                pe[x, p, here, :] = jnp.where(marks_e[x] == p, base_e + rate[p], base_e)

    copies = []
    for t in range(8):
        here = pl.ds(8 + 8 * t, 8)
        above, below = pl.ds(7 + 8 * t, 8), pl.ds(9 + 8 * t, 8)
        for x in range(2):
            ms = [pm[x, p, here, :] for p in range(NP)]
            sm = 6.0 + sum(m * m for m in ms)
            marks_m = lm[x, here, :]
            for p in range(NP):
                m, e, other = ms[p], pe[x, p, here, :], pm[1 - x, p, here, :]
                west = jnp.where(first_lane, e, pltpu.roll(m, 1, 1))
                east = jnp.where(last_lane, e, pltpu.roll(m, 127, 1))
                lap = (pm[x, p, above, :] + pm[x, p, below, :]) + (west + east) + (other + other)
                change = lap - sm * m
                change = jnp.where(marks_m == p, change + 1.0, change)
                out[p, x, 8 * t : 8 * t + 8, :] = m + rate[p] * change
        if t in (2, 5, 7):
            part = (2, 5, 7).index(t)
            rows = pl.ds(24 * part, 24 if t < 7 else 16)
            copies.append(pltpu.make_async_copy(out.at[:, :, rows, :], out_hbm.at[:, :, rows, :], sems.at[part]))
            copies[-1].start()
    for copy in copies:
        copy.wait()


def exchanged(cells, pairs):
    width = lax.axis_size("gz")
    flat = [(i * width + j, k * width + l) for (i, j), (k, l) in pairs]
    return lax.ppermute(cells, ("gy", "gz"), flat + [(b, a) for a, b in flat])


def paired(cells, axis, odd):
    count = lax.axis_size(axis)
    return lax.all_gather(cells, axis, axis_index_groups=[[i, (i + 1) % count] for i in range(odd, count, 2)])


def shards(coarse, labels, mobility):
    coarse = coarse.reshape(NP, CR, CC)
    vmem = pl.BlockSpec(memory_space=pltpu.VMEM)
    hbm = pl.BlockSpec(memory_space=pltpu.HBM)
    tile = lambda *shape: pltpu.VMEM(shape + (128,), F32)
    to_a, to_b, rates = pl.pallas_call(
        strips_kernel,
        out_shape=(tile(MROWS), tile(MROWS), tile(8)),
        in_specs=[hbm, hbm, hbm],
        out_specs=(vmem,) * 3,
        scratch_shapes=[
            pltpu.VMEM((NP, 8, CC), F32),
            pltpu.VMEM((NP, 8, CC), F32),
            pltpu.VMEM((2, 16, FC), jnp.int32),
            pltpu.SMEM((NP,), F32),
            tile(MROWS),
            tile(MROWS),
            pltpu.SemaphoreType.DMA((5,)),
        ],
        compiler_params=pltpu.CompilerParams(vmem_limit_bytes=8 << 20),
        cost_estimate=pl.CostEstimate(flops=20000, bytes_accessed=200000, transcendentals=0),
        name="strips",
    )(*(pltpu.with_memory_space_constraint(x, pltpu.HBM) for x in (coarse, labels, mobility)))
    rows, cols = lax.axis_size("gy"), lax.axis_size("gz")
    yb = exchanged(to_b, [((i, j), ((i + 1) % rows, j)) for i in range(1, rows, 2) for j in range(cols)])
    ya = paired(to_a, "gy", 0)
    columns = pl.pallas_call(
        columns_kernel,
        out_shape=tile(16),
        in_specs=[vmem, vmem],
        out_specs=vmem,
        compiler_params=pltpu.CompilerParams(vmem_limit_bytes=8 << 20),
        cost_estimate=pl.CostEstimate(flops=20000, bytes_accessed=200000, transcendentals=0),
        name="columns",
    )(coarse, labels)
    sides = pl.pallas_call(
        sides_kernel,
        out_shape=tile(24),
        in_specs=[vmem] * 3,
        out_specs=vmem,
        compiler_params=pltpu.CompilerParams(vmem_limit_bytes=8 << 20),
        cost_estimate=pl.CostEstimate(flops=20000, bytes_accessed=40000, transcendentals=0),
        name="sides",
    )(columns, ya, yb)
    last = cols - 2
    first_rows = (0,)
    za0 = exchanged(sides, [((i, j), (i, j + 1)) for i in range(rows) for j in range(0, cols, 2) if j < last or i in first_rows])
    zb = paired(sides, "gz", 1)
    sides, zb = lax.optimization_barrier((sides, zb))
    za1 = exchanged(sides, [((i, last), (i, last + 1)) for i in range(rows) if i not in first_rows])
    return pl.pallas_call(
        relax_kernel,
        out_shape=jax.ShapeDtypeStruct((NP, 2, FR, FC), F32),
        in_specs=[vmem] * 8,
        out_specs=hbm,
        scratch_shapes=[
            tile(NP * 48),
            tile(NP, 48),
            tile(NP, 48),
            tile(NP, 88),
            tile(NP, 88),
            tile(2, 80),
            tile(2, 80),
            tile(2, NP, 80),
            tile(2, NP, 80),
            tile(NP, 2, FR),
            pltpu.SemaphoreType.DMA((3,)),
        ],
        compiler_params=pltpu.CompilerParams(vmem_limit_bytes=16 << 20),
        cost_estimate=pl.CostEstimate(flops=8000000, bytes_accessed=900000, transcendentals=0),
        name="relax",
    )(rates, coarse, labels, ya, yb, za0, za1, zb)


def solution(mesh):
    in_specs = (P(None, None, "gy", "gz"), P(None, "gy", "gz"), P())
    out_specs = P(None, None, "gy", "gz")
    return jax.shard_map(shards, mesh=mesh, in_specs=in_specs, out_specs=out_specs, check_vma=False)
```

time: 29.3 us -> 25.9 us (0.88)
  local copies, waits for them, and re-layouts: 2.44 us -> 0.01 us
  blocking collectives: 16.9 us -> 15 us
  starting transfers between devices: 7.17 us -> 7.69 us
  Pallas kernels: 2.46 us -> 2.95 us
    unnamed x10 -> x4, local copies, waits for them, and re-layouts: 2.39 us -> 0.01 us
    all_gather x2, blocking collectives: 16.9 us -> 15 us  [paired(): lax.all_gather(cells, axis, axis_index_groups=[[i, (i + 1) % count] for i...]
    pallas_call x1 -> x3, Pallas kernels: 0.18 us -> 1.23 us  [the longest x1 0.98 us: shards(): pl.pallas_call(strips_kernel, out_shape=(tile(MROWS), tile(MROWS), tile(8...]
    pallas_call x1, Pallas kernels: 2.29 us -> 1.72 us  [shards(): pl.pallas_call(relax_kernel, out_shape=jax.ShapeDtypeStruct((NP, 2, FR, F...]
    ppermute x2 -> x3, starting transfers between devices: 7.17 us -> 7.69 us  [exchanged(): return lax.ppermute(cells, ('gy', 'gz'), flat + [(b, a) for a, b in flat])]
  transfers between devices with their start and end apart: 2 -> 3, of which waited for: 0 -> 0; matrix products, arithmetic and copies ran while one was open for 0% -> 0% of each run, Pallas kernels for 0% -> 1%
where the time goes in v2:
time: 25.9 us; the launch traced here: 25.8 us
  blocking collectives  15 us (58%)
  starting transfers between devices  7.69 us (30%)
  Pallas kernels  2.95 us (11%)
    all_gather x2, blocking collectives, paired(): lax.all_gather(cells, axis, axis_index_groups=[[i, (i + 1) % count] for i...  15 us
    ppermute x3, starting transfers between devices, exchanged(): return lax.ppermute(cells, ('gy', 'gz'), flat + [(b, a) for a, b in flat])  7.69 us
    pallas_call x1, Pallas kernels, shards(): pl.pallas_call(relax_kernel, out_shape=jax.ShapeDtypeStruct((NP, 2, FR, F...  1.72 us
    pallas_call x1, Pallas kernels, shards(): pl.pallas_call(strips_kernel, out_shape=(tile(MROWS), tile(MROWS), tile(8...  0.98 us
  transfers between devices with their start and end apart: 3, of which 0 were waited for; matrix products, arithmetic and copies ran while one was open for 0% of the time, Pallas kernels for 1%

profile of v2, /device:TPU:1, one launch (start us, length us, event | category | flops | bytes accessed | tf_op | source)
XLA Modules:
  0.0 25.8 jit_solution(2030814267353366769)
XLA Ops:
  0.0 0.0 copy-start
  0.0 0.0 copy-start.1
  0.0 1.0 %strips.1 = (f32[16,128]{1,0:T(8,128)S(1)}, f32[16,128]{1,0:T(8,128)S(1)}, f32[8,128]{1,0:T(8,128)S(1)}) custom-call(f32[8,32,64]{2,1,0:T(8,128)} %bitcast.3, s32[2,64,128]{2,1,0:T(8,128)} %labels.3, f32[8]{0:T(128)} %mobility_hbm.1), custom_call_target="tpu_custom_call" | custom-call | flops 20000 | bytes 200000 | tf_op jit(solution)/shard_map/strips/pallas_call | solution.py:211
  1.0 4.6 %collective-permute-start = (f32[16,128]{1,0:T(8,128)S(1)}, f32[16,128]{1,0:T(8,128)S(1)}, u32[]{:S(2)}, u32[]{:S(2)}) collective-permute-start(f32[16,128]{1,0:T(8,128)S(1)} %get-tuple-element.12), channel_id=1, source_target_pairs={{16,32},{17,33},{18,34},{19,35},{20,36},{21,37},{22,38},{23,39},{2... | collective-permute-start | bytes 24584 | tf_op jit(solution)/shard_map/ppermute | solution.py:198
  5.6 0.0 copy-done
  5.6 0.0 copy-done.1
  5.6 0.2 columns.1
  5.8 5.7 %all-gather = f32[32,128]{1,0:T(8,128)S(1)} all-gather(f32[16,128]{1,0:T(8,128)S(1)} %get-tuple-element.11), channel_id=2, replica_groups={{0,16},{32,48},{64,80},{96,112},{128,144},{160,176},{192,208},{224,240}..., dimensions={0}, use_global_device_ids=true | all-gather | bytes 24576 | tf_op jit(solution)/shard_map/all_gather | solution.py:203
  11.5 0.0 collective-permute-done.yb
  11.5 0.1 sides.1
  11.6 2.4 %collective-permute-start.1 = (f32[24,128]{1,0:T(8,128)S(1)}, f32[24,128]{1,0:T(8,128)S(1)}, u32[]{:S(2)}, u32[]{:S(2)}) collective-permute-start(f32[24,128]{1,0:T(8,128)S(1)} %sides.1), channel_id=1, source_target_pairs={{0,1},{2,3},{4,5},{6,7},{8,9},{10,11},{12,13},{14,15},{16,17},{18,... | collective-permute-start | bytes 36872 | tf_op jit(solution)/shard_map/ppermute | solution.py:198
  14.0 9.3 %all-gather.1 = f32[48,128]{1,0:T(8,128)S(1)} all-gather(f32[24,128]{1,0:T(8,128)S(1)} %sides.1), channel_id=3, replica_groups={{1,2},{3,4},{5,6},{7,8},{9,10},{11,12},{13,14},{15,0},{17,18},{19,20},{..., dimensions={0}, use_global_device_ids=true | all-gather | bytes 36864 | tf_op jit(solution)/shard_map/all_gather | solution.py:203
  23.4 0.7 %collective-permute-start.2 = (f32[24,128]{1,0:T(8,128)S(1)}, f32[24,128]{1,0:T(8,128)S(1)}, u32[]{:S(2)}, u32[]{:S(2)}) collective-permute-start(f32[24,128]{1,0:T(8,128)S(1)} %sides.1), channel_id=1, source_target_pairs={{30,31},{46,47},{62,63},{78,79},{94,95},{110,111},{126,127},{142,1... | collective-permute-start | bytes 36872 | tf_op jit(solution)/shard_map/ppermute | solution.py:198
  24.0 0.0 collective-permute-done.1.za0
  24.0 0.0 collective-permute-done.2.za1
  24.0 1.7 %relax.1 = f32[8,2,64,128]{3,2,1,0:T(8,128)} custom-call(f32[8,128]{1,0:T(8,128)S(1)} %get-tuple-element.10.rates, f32[8,32,64]{2,1,0:T(8,128)S(1)} %bitcast.5, s32[2,64,128]{2,1,0:T(8,128)S(1)} %copy-done.1, f32[2,16,128]{2,1,0:T(8,128)S(1)} %bitcast.7, f32[16,128]{1,0:T(8,128)S(1)} %collective-permute-done.yb, f32[24,128]{1,0:T(8,128)S(1)} %collective-permute-done.1.za0, ...), custom_call_target="tpu_custom_call" | custom-call | flops 8000000 | bytes 900000 | tf_op jit(solution)/shard_map/relax/pallas_call | solution.py:256
Async XLA Ops:
  0.0 5.6 %copy-start = (f32[8,1,32,64]{3,2,1,0:T(8,128)S(1)}, f32[8,1,32,64]{3,2,1,0:T(8,128)}, u32[]{:S(2)}) copy-start(f32[8,1,32,64]{3,2,1,0:T(8,128)} %param.3) | copy-start | bytes 196612
  0.0 5.6 %copy-start.1 = (s32[2,64,128]{2,1,0:T(8,128)S(1)}, s32[2,64,128]{2,1,0:T(8,128)}, u32[]{:S(2)}) copy-start(s32[2,64,128]{2,1,0:T(8,128)} %labels.3) | copy-start | bytes 196612
  1.0 10.5 %collective-permute-start = (f32[16,128]{1,0:T(8,128)S(1)}, f32[16,128]{1,0:T(8,128)S(1)}, u32[]{:S(2)}, u32[]{:S(2)}) collective-permute-start(f32[16,128]{1,0:T(8,128)S(1)} %get-tuple-element.12), channel_id=1, source_target_pairs={{16,32},{17,33},{18,34},{19,35},{20,36},{21,37},{22,38},{23,39},{2... | collective-permute-start | bytes 24584 | tf_op jit(solution)/shard_map/ppermute | solution.py:198
  11.6 12.5 %collective-permute-start.1 = (f32[24,128]{1,0:T(8,128)S(1)}, f32[24,128]{1,0:T(8,128)S(1)}, u32[]{:S(2)}, u32[]{:S(2)}) collective-permute-start(f32[24,128]{1,0:T(8,128)S(1)} %sides.1), channel_id=1, source_target_pairs={{0,1},{2,3},{4,5},{6,7},{8,9},{10,11},{12,13},{14,15},{16,17},{18,... | collective-permute-start | bytes 36872 | tf_op jit(solution)/shard_map/ppermute | solution.py:198
  23.4 0.7 %collective-permute-start.2 = (f32[24,128]{1,0:T(8,128)S(1)}, f32[24,128]{1,0:T(8,128)S(1)}, u32[]{:S(2)}, u32[]{:S(2)}) collective-permute-start(f32[24,128]{1,0:T(8,128)S(1)} %sides.1), channel_id=1, source_target_pairs={{30,31},{46,47},{62,63},{78,79},{94,95},{110,111},{126,127},{142,1... | collective-permute-start | bytes 36872 | tf_op jit(solution)/shard_map/ppermute | solution.py:198

commit v3 on v2

--- a/solution.py
+++ b/solution.py
@@ -21,7 +21,7 @@
     return lax.axis_index("gy") % 2 == 0, lax.axis_index("gz") % 2 == 0
 
 
-def strips_kernel(coarse_hbm, labels_hbm, mobility_hbm, to_a, to_b, rates, top, bottom, marks, mobility, low, high, sems):
+def strips_kernel(coarse_hbm, labels_hbm, mobility_hbm, to_a, to_b, rates, top, bottom, marks, mobility, low, high, second, sems):
     copies = [
         pltpu.make_async_copy(src, dst, sems.at[i])
         for i, (src, dst) in enumerate(
@@ -42,7 +42,8 @@
     for row, block, strip in ((0, top, low), (6, bottom, high)):
         for p in range(NP):
             strip[p : p + 1, 0:CC] = block[p, row : row + 1, :]
-            strip[p : p + 1, CC : 2 * CC] = block[p, row + 1 : row + 2, :]
+            second[p : p + 1, 0:CC] = block[p, row + 1 : row + 2, :]
+        strip[0:8, :] = jnp.where(lanes(8) < CC, strip[0:8, :], pltpu.roll(second[...], CC, 1))
         for x in range(2):
             strip[8 + x : 9 + x, :] = marks[x, 15 * (row // 6) : 15 * (row // 6) + 1, :].astype(F32)
         strip[10:16, :] = jnp.zeros((6, 128), F32)
@@ -52,7 +53,7 @@
         rates[p : p + 1, :] = jnp.full((1, 128), STEP * mobility[p], F32)
 
 
-def columns_kernel(coarse, labels, sides):
+def write_columns(coarse, labels, sides):
     lane = lanes(8)
     first, last = jnp.zeros((8, 128), F32), jnp.zeros((8, 128), F32)
     for g in range(4):
@@ -71,13 +72,28 @@
     sides[8:16, :] = last
 
 
+def columns_kernel(coarse, labels, sides):
+    @pl.when(lax.axis_index("gy") != 0)
+    def _():
+        write_columns(coarse, labels, sides)
+
+
 def picked(ya0, ya1, yb):
     y_even, _ = parities()
     return jnp.where(y_even, yb, ya0), jnp.where(y_even, ya1, yb)
 
 
-def sides_kernel(columns, ya, yb, sides):
-    sides[0:16, :] = columns[...]
+def sides_kernel(coarse, labels, columns, ya, yb, sides):
+    row = lax.axis_index("gy")
+
+    @pl.when(row != 0)
+    def _():
+        sides[0:16, :] = columns[...]
+
+    @pl.when(row == 0)
+    def _():
+        write_columns(coarse, labels, sides)
+
     lane = lanes(8)
     ends = jnp.zeros((8, 128), F32)
     for j, strip in enumerate(picked(ya[0, 0:8], ya[1, 0:8], yb[0:8])):
@@ -156,7 +172,7 @@
         marks_m = [lm[x, here, :] for x in range(2)]
         marks_e = [le[x, here, :] for x in range(2)]
         for p in range(NP):
-            m, e = ms[p], es[p]
+            m, e = fm[p, here, :], fe[p, here, :]
             west = jnp.where(first_lane, e, pltpu.roll(m, 1, 1))
             east = jnp.where(last_lane, e, pltpu.roll(m, 127, 1))
             lap = (fm[p, above, :] + fm[p, below, :]) + (west + east)
@@ -220,6 +236,7 @@
             pltpu.SMEM((NP,), F32),
             tile(MROWS),
             tile(MROWS),
+            tile(8),
             pltpu.SemaphoreType.DMA((5,)),
         ],
         compiler_params=pltpu.CompilerParams(vmem_limit_bytes=8 << 20),
@@ -241,12 +258,12 @@
     sides = pl.pallas_call(
         sides_kernel,
         out_shape=tile(24),
-        in_specs=[vmem] * 3,
+        in_specs=[vmem] * 5,
         out_specs=vmem,
         compiler_params=pltpu.CompilerParams(vmem_limit_bytes=8 << 20),
         cost_estimate=pl.CostEstimate(flops=20000, bytes_accessed=40000, transcendentals=0),
         name="sides",
-    )(columns, ya, yb)
+    )(coarse, labels, columns, ya, yb)
     last = cols - 2
     first_rows = (0,)
     za0 = exchanged(sides, [((i, j), (i, j + 1)) for i in range(rows) for j in range(0, cols, 2) if j < last or i in first_rows])

time: 25.9 us -> 25.9 us (level)
  no operation moved by 1% of the time
where the time goes in v3:
time: 25.9 us; the launch traced here: 25.7 us
  blocking collectives  15 us (58%)
  starting transfers between devices  7.69 us (30%)
  Pallas kernels  2.95 us (11%)
    all_gather x2, blocking collectives, paired(): lax.all_gather(cells, axis, axis_index_groups=[[i, (i + 1) % count] for i...  15 us
    ppermute x3, starting transfers between devices, exchanged(): return lax.ppermute(cells, ('gy', 'gz'), flat + [(b, a) for a, b in flat])  7.69 us
    pallas_call x1, Pallas kernels, shards(): pl.pallas_call(relax_kernel, out_shape=jax.ShapeDtypeStruct((NP, 2, FR, F...  1.72 us
    pallas_call x1, Pallas kernels, shards(): pl.pallas_call(strips_kernel, out_shape=(tile(MROWS), tile(MROWS), tile(8...  0.97 us
  transfers between devices with their start and end apart: 3, of which 0 were waited for; matrix products, arithmetic and copies ran while one was open for 0% of the time, Pallas kernels for 1%

profile of v3, /device:TPU:1, one launch (start us, length us, event | category | flops | bytes accessed | tf_op | source)
XLA Modules:
  0.0 25.7 jit_solution(250985517818098888)
XLA Ops:
  0.0 0.0 copy-start
  0.0 0.0 copy-start.1
  0.0 1.0 %strips.1 = (f32[16,128]{1,0:T(8,128)S(1)}, f32[16,128]{1,0:T(8,128)S(1)}, f32[8,128]{1,0:T(8,128)S(1)}) custom-call(f32[8,32,64]{2,1,0:T(8,128)} %bitcast.3, s32[2,64,128]{2,1,0:T(8,128)} %labels.5, f32[8]{0:T(128)} %mobility_hbm.1), custom_call_target="tpu_custom_call" | custom-call | flops 20000 | bytes 200000 | tf_op jit(solution)/shard_map/strips/pallas_call | solution.py:227
  1.0 4.6 %collective-permute-start = (f32[16,128]{1,0:T(8,128)S(1)}, f32[16,128]{1,0:T(8,128)S(1)}, u32[]{:S(2)}, u32[]{:S(2)}) collective-permute-start(f32[16,128]{1,0:T(8,128)S(1)} %get-tuple-element.12), channel_id=1, source_target_pairs={{16,32},{17,33},{18,34},{19,35},{20,36},{21,37},{22,38},{23,39},{2... | collective-permute-start | bytes 24584 | tf_op jit(solution)/shard_map/ppermute | solution.py:214
  5.6 0.0 copy-done
  5.6 0.0 copy-done.1
  5.6 0.2 columns.1
  5.8 5.5 %all-gather = f32[32,128]{1,0:T(8,128)S(1)} all-gather(f32[16,128]{1,0:T(8,128)S(1)} %get-tuple-element.11), channel_id=2, replica_groups={{0,16},{32,48},{64,80},{96,112},{128,144},{160,176},{192,208},{224,240}..., dimensions={0}, use_global_device_ids=true | all-gather | bytes 24576 | tf_op jit(solution)/shard_map/all_gather | solution.py:219
  11.3 0.0 collective-permute-done.yb
  11.3 0.1 sides.1
  11.4 2.4 %collective-permute-start.1 = (f32[24,128]{1,0:T(8,128)S(1)}, f32[24,128]{1,0:T(8,128)S(1)}, u32[]{:S(2)}, u32[]{:S(2)}) collective-permute-start(f32[24,128]{1,0:T(8,128)S(1)} %sides.1), channel_id=1, source_target_pairs={{0,1},{2,3},{4,5},{6,7},{8,9},{10,11},{12,13},{14,15},{16,17},{18,... | collective-permute-start | bytes 36872 | tf_op jit(solution)/shard_map/ppermute | solution.py:214
  13.9 9.4 %all-gather.1 = f32[48,128]{1,0:T(8,128)S(1)} all-gather(f32[24,128]{1,0:T(8,128)S(1)} %sides.1), channel_id=3, replica_groups={{1,2},{3,4},{5,6},{7,8},{9,10},{11,12},{13,14},{15,0},{17,18},{19,20},{..., dimensions={0}, use_global_device_ids=true | all-gather | bytes 36864 | tf_op jit(solution)/shard_map/all_gather | solution.py:219
  23.3 0.7 %collective-permute-start.2 = (f32[24,128]{1,0:T(8,128)S(1)}, f32[24,128]{1,0:T(8,128)S(1)}, u32[]{:S(2)}, u32[]{:S(2)}) collective-permute-start(f32[24,128]{1,0:T(8,128)S(1)} %sides.1), channel_id=1, source_target_pairs={{30,31},{46,47},{62,63},{78,79},{94,95},{110,111},{126,127},{142,1... | collective-permute-start | bytes 36872 | tf_op jit(solution)/shard_map/ppermute | solution.py:214
  24.0 0.0 collective-permute-done.1.za0
  24.0 0.0 collective-permute-done.2.za1
  24.0 1.7 %relax.1 = f32[8,2,64,128]{3,2,1,0:T(8,128)} custom-call(f32[8,128]{1,0:T(8,128)S(1)} %get-tuple-element.10.rates, f32[8,32,64]{2,1,0:T(8,128)S(1)} %bitcast.6, s32[2,64,128]{2,1,0:T(8,128)S(1)} %copy-done.1, f32[2,16,128]{2,1,0:T(8,128)S(1)} %bitcast.8, f32[16,128]{1,0:T(8,128)S(1)} %collective-permute-done.yb, f32[24,128]{1,0:T(8,128)S(1)} %collective-permute-done.1.za0, ...), custom_call_target="tpu_custom_call" | custom-call | flops 8000000 | bytes 900000 | tf_op jit(solution)/shard_map/relax/pallas_call | solution.py:273
Async XLA Ops:
  0.0 5.6 %copy-start = (f32[8,1,32,64]{3,2,1,0:T(8,128)S(1)}, f32[8,1,32,64]{3,2,1,0:T(8,128)}, u32[]{:S(2)}) copy-start(f32[8,1,32,64]{3,2,1,0:T(8,128)} %param.3) | copy-start | bytes 196612
  0.0 5.6 %copy-start.1 = (s32[2,64,128]{2,1,0:T(8,128)S(1)}, s32[2,64,128]{2,1,0:T(8,128)}, u32[]{:S(2)}) copy-start(s32[2,64,128]{2,1,0:T(8,128)} %labels.5) | copy-start | bytes 196612
  1.0 10.3 %collective-permute-start = (f32[16,128]{1,0:T(8,128)S(1)}, f32[16,128]{1,0:T(8,128)S(1)}, u32[]{:S(2)}, u32[]{:S(2)}) collective-permute-start(f32[16,128]{1,0:T(8,128)S(1)} %get-tuple-element.12), channel_id=1, source_target_pairs={{16,32},{17,33},{18,34},{19,35},{20,36},{21,37},{22,38},{23,39},{2... | collective-permute-start | bytes 24584 | tf_op jit(solution)/shard_map/ppermute | solution.py:214
  11.4 12.6 %collective-permute-start.1 = (f32[24,128]{1,0:T(8,128)S(1)}, f32[24,128]{1,0:T(8,128)S(1)}, u32[]{:S(2)}, u32[]{:S(2)}) collective-permute-start(f32[24,128]{1,0:T(8,128)S(1)} %sides.1), channel_id=1, source_target_pairs={{0,1},{2,3},{4,5},{6,7},{8,9},{10,11},{12,13},{14,15},{16,17},{18,... | collective-permute-start | bytes 36872 | tf_op jit(solution)/shard_map/ppermute | solution.py:214
  23.3 0.7 %collective-permute-start.2 = (f32[24,128]{1,0:T(8,128)S(1)}, f32[24,128]{1,0:T(8,128)S(1)}, u32[]{:S(2)}, u32[]{:S(2)}) collective-permute-start(f32[24,128]{1,0:T(8,128)S(1)} %sides.1), channel_id=1, source_target_pairs={{30,31},{46,47},{62,63},{78,79},{94,95},{110,111},{126,127},{142,1... | collective-permute-start | bytes 36872 | tf_op jit(solution)/shard_map/ppermute | solution.py:214

commit v4 on v2

--- a/solution.py
+++ b/solution.py
@@ -77,15 +77,15 @@
 
 
 def sides_kernel(columns, ya, yb, sides):
-    sides[0:16, :] = columns[...]
     lane = lanes(8)
-    ends = jnp.zeros((8, 128), F32)
+    first, last = columns[0:8, :], columns[8:16, :]
     for j, strip in enumerate(picked(ya[0, 0:8], ya[1, 0:8], yb[0:8])):
         for i in range(2):
-            at = 64 + 16 * j + 8 * i
-            ends = jnp.where(lane // 2 == at // 2, pltpu.roll(strip, (at - 62 - 64 * i) % 128, 1), ends)
-            ends = jnp.where(lane // 2 == at // 2 + 1, pltpu.roll(strip, (at + 2 - 64 * i) % 128, 1), ends)
-    sides[16:24, :] = ends
+            at = 50 + 4 * j + 2 * i
+            first = jnp.where(lane // 2 == at // 2, pltpu.roll(strip, (at - 64 * i) % 128, 1), first)
+            last = jnp.where(lane // 2 == at // 2, pltpu.roll(strip, (at - 62 - 64 * i) % 128, 1), last)
+    sides[0:8, :] = first
+    sides[8:16, :] = last
 
 
 def z_weights():
@@ -120,10 +120,10 @@
             le[k % 2, rows, :] = jnp.where(first_lane, pltpu.roll(west, 128 - at, 1), pltpu.roll(east, 127 - at, 1))
     for p in range(NP):
         pad[48 * p + 8 : 48 * p + 8 + CR, 0:CC] = coarse[p]
-    ends = jnp.where(lane8 % 4 < 2, left[16:24], right[16:24])
     for j, strip in enumerate((low, high)):
         for i in range(2):
-            beside = pltpu.roll(ends, (-16 * j - 8 * i) % 128, 1)
+            at = 50 + 4 * j + 2 * i
+            beside = jnp.where(lane8 < 66, pltpu.roll(west, 64 - at, 1), pltpu.roll(east, 66 - at, 1))
             cells = pltpu.roll(strip[0:8], CC, 1) if i else strip[0:8]
             pad[pl.ds(6 + 34 * j + i, NP, stride=48), :] = jnp.where(lane8 < CC, cells, beside)
 
@@ -240,7 +240,7 @@
     )(coarse, labels)
     sides = pl.pallas_call(
         sides_kernel,
-        out_shape=tile(24),
+        out_shape=tile(MROWS),
         in_specs=[vmem] * 3,
         out_specs=vmem,
         compiler_params=pltpu.CompilerParams(vmem_limit_bytes=8 << 20),
@@ -251,7 +251,7 @@
     first_rows = (0,)
     za0 = exchanged(sides, [((i, j), (i, j + 1)) for i in range(rows) for j in range(0, cols, 2) if j < last or i in first_rows])
     zb = paired(sides, "gz", 1)
-    sides, zb = lax.optimization_barrier((sides, zb))
+    sides, zb, za0 = lax.optimization_barrier((sides, zb, za0))
     za1 = exchanged(sides, [((i, last), (i, last + 1)) for i in range(rows) if i not in first_rows])
     return pl.pallas_call(
         relax_kernel,

time: 25.9 us -> 25.9 us (level)
  no operation moved by 1% of the time
where the time goes in v4:
time: 25.9 us; the launch traced here: 25.7 us
  blocking collectives  15 us (58%)
  starting transfers between devices  7.69 us (30%)
  Pallas kernels  2.94 us (11%)
    all_gather x2, blocking collectives, paired(): lax.all_gather(cells, axis, axis_index_groups=[[i, (i + 1) % count] for i...  15 us
    ppermute x3, starting transfers between devices, exchanged(): return lax.ppermute(cells, ('gy', 'gz'), flat + [(b, a) for a, b in flat])  7.69 us
    pallas_call x1, Pallas kernels, shards(): pl.pallas_call(relax_kernel, out_shape=jax.ShapeDtypeStruct((NP, 2, FR, F...  1.72 us
    pallas_call x1, Pallas kernels, shards(): pl.pallas_call(strips_kernel, out_shape=(tile(MROWS), tile(MROWS), tile(8...  0.98 us
  transfers between devices with their start and end apart: 3, of which 0 were waited for; matrix products, arithmetic and copies ran while one was open for 0% of the time, Pallas kernels for 1%

profile of v4, /device:TPU:1, one launch (start us, length us, event | category | flops | bytes accessed | tf_op | source)
XLA Modules:
  0.0 25.7 jit_solution(7327818771119738734)
XLA Ops:
  0.0 0.0 copy-start
  0.0 0.0 copy-start.1
  0.0 1.0 %strips.1 = (f32[16,128]{1,0:T(8,128)S(1)}, f32[16,128]{1,0:T(8,128)S(1)}, f32[8,128]{1,0:T(8,128)S(1)}) custom-call(f32[8,32,64]{2,1,0:T(8,128)} %bitcast.3, s32[2,64,128]{2,1,0:T(8,128)} %labels.3, f32[8]{0:T(128)} %mobility_hbm.1), custom_call_target="tpu_custom_call" | custom-call | flops 20000 | bytes 200000 | tf_op jit(solution)/shard_map/strips/pallas_call | solution.py:211
  1.0 4.6 %collective-permute-start = (f32[16,128]{1,0:T(8,128)S(1)}, f32[16,128]{1,0:T(8,128)S(1)}, u32[]{:S(2)}, u32[]{:S(2)}) collective-permute-start(f32[16,128]{1,0:T(8,128)S(1)} %get-tuple-element.13), channel_id=1, source_target_pairs={{16,32},{17,33},{18,34},{19,35},{20,36},{21,37},{22,38},{23,39},{2... | collective-permute-start | bytes 24584 | tf_op jit(solution)/shard_map/ppermute | solution.py:198
  5.6 0.0 copy-done
  5.6 0.0 copy-done.1
  5.6 0.2 columns.1
  5.8 5.7 %all-gather = f32[32,128]{1,0:T(8,128)S(1)} all-gather(f32[16,128]{1,0:T(8,128)S(1)} %get-tuple-element.12), channel_id=2, replica_groups={{0,16},{32,48},{64,80},{96,112},{128,144},{160,176},{192,208},{224,240}..., dimensions={0}, use_global_device_ids=true | all-gather | bytes 24576 | tf_op jit(solution)/shard_map/all_gather | solution.py:203
  11.5 0.0 collective-permute-done.yb
  11.5 0.1 sides.1
  11.6 2.4 %collective-permute-start.1 = (f32[16,128]{1,0:T(8,128)S(1)}, f32[16,128]{1,0:T(8,128)S(1)}, u32[]{:S(2)}, u32[]{:S(2)}) collective-permute-start(f32[16,128]{1,0:T(8,128)S(1)} %sides.1), channel_id=1, source_target_pairs={{0,1},{2,3},{4,5},{6,7},{8,9},{10,11},{12,13},{14,15},{16,17},{18,... | collective-permute-start | bytes 24584 | tf_op jit(solution)/shard_map/ppermute | solution.py:198
  14.0 9.3 %all-gather.1 = f32[32,128]{1,0:T(8,128)S(1)} all-gather(f32[16,128]{1,0:T(8,128)S(1)} %sides.1), channel_id=3, replica_groups={{1,2},{3,4},{5,6},{7,8},{9,10},{11,12},{13,14},{15,0},{17,18},{19,20},{..., dimensions={0}, use_global_device_ids=true | all-gather | bytes 24576 | tf_op jit(solution)/shard_map/all_gather | solution.py:203
  23.3 0.0 collective-permute-done.1.za0
  23.3 0.7 %collective-permute-start.2 = (f32[16,128]{1,0:T(8,128)S(1)}, f32[16,128]{1,0:T(8,128)S(1)}, u32[]{:S(2)}, u32[]{:S(2)}) collective-permute-start(f32[16,128]{1,0:T(8,128)S(1)} %sides.1), channel_id=1, source_target_pairs={{30,31},{46,47},{62,63},{78,79},{94,95},{110,111},{126,127},{142,1... | collective-permute-start | bytes 24584 | tf_op jit(solution)/shard_map/ppermute | solution.py:198
  24.0 0.0 collective-permute-done.2.za1
  24.0 1.7 %relax.1 = f32[8,2,64,128]{3,2,1,0:T(8,128)} custom-call(f32[8,128]{1,0:T(8,128)S(1)} %get-tuple-element.11.rates, f32[8,32,64]{2,1,0:T(8,128)S(1)} %bitcast.5, s32[2,64,128]{2,1,0:T(8,128)S(1)} %copy-done.1, f32[2,16,128]{2,1,0:T(8,128)S(1)} %bitcast.7, f32[16,128]{1,0:T(8,128)S(1)} %collective-permute-done.yb, f32[16,128]{1,0:T(8,128)S(1)} %collective-permute-done.1.za0, ...), custom_call_target="tpu_custom_call" | custom-call | flops 8000000 | bytes 900000 | tf_op jit(solution)/shard_map/relax/pallas_call | solution.py:256
Async XLA Ops:
  0.0 5.6 %copy-start = (f32[8,1,32,64]{3,2,1,0:T(8,128)S(1)}, f32[8,1,32,64]{3,2,1,0:T(8,128)}, u32[]{:S(2)}) copy-start(f32[8,1,32,64]{3,2,1,0:T(8,128)} %param.3) | copy-start | bytes 196612
  0.0 5.6 %copy-start.1 = (s32[2,64,128]{2,1,0:T(8,128)S(1)}, s32[2,64,128]{2,1,0:T(8,128)}, u32[]{:S(2)}) copy-start(s32[2,64,128]{2,1,0:T(8,128)} %labels.3) | copy-start | bytes 196612
  1.0 10.5 %collective-permute-start = (f32[16,128]{1,0:T(8,128)S(1)}, f32[16,128]{1,0:T(8,128)S(1)}, u32[]{:S(2)}, u32[]{:S(2)}) collective-permute-start(f32[16,128]{1,0:T(8,128)S(1)} %get-tuple-element.13), channel_id=1, source_target_pairs={{16,32},{17,33},{18,34},{19,35},{20,36},{21,37},{22,38},{23,39},{2... | collective-permute-start | bytes 24584 | tf_op jit(solution)/shard_map/ppermute | solution.py:198
  11.6 11.8 %collective-permute-start.1 = (f32[16,128]{1,0:T(8,128)S(1)}, f32[16,128]{1,0:T(8,128)S(1)}, u32[]{:S(2)}, u32[]{:S(2)}) collective-permute-start(f32[16,128]{1,0:T(8,128)S(1)} %sides.1), channel_id=1, source_target_pairs={{0,1},{2,3},{4,5},{6,7},{8,9},{10,11},{12,13},{14,15},{16,17},{18,... | collective-permute-start | bytes 24584 | tf_op jit(solution)/shard_map/ppermute | solution.py:198
  23.3 0.7 %collective-permute-start.2 = (f32[16,128]{1,0:T(8,128)S(1)}, f32[16,128]{1,0:T(8,128)S(1)}, u32[]{:S(2)}, u32[]{:S(2)}) collective-permute-start(f32[16,128]{1,0:T(8,128)S(1)} %sides.1), channel_id=1, source_target_pairs={{30,31},{46,47},{62,63},{78,79},{94,95},{110,111},{126,127},{142,1... | collective-permute-start | bytes 24584 | tf_op jit(solution)/shard_map/ppermute | solution.py:198

commit v5 on v4

--- a/solution.py
+++ b/solution.py
@@ -21,7 +21,7 @@
     return lax.axis_index("gy") % 2 == 0, lax.axis_index("gz") % 2 == 0
 
 
-def strips_kernel(coarse_hbm, labels_hbm, mobility_hbm, to_a, to_b, rates, top, bottom, marks, mobility, low, high, sems):
+def strips_kernel(coarse_hbm, labels_hbm, mobility_hbm, to_a, to_b, rates, top, bottom, marks, mobility, low, high, second, sems):
     copies = [
         pltpu.make_async_copy(src, dst, sems.at[i])
         for i, (src, dst) in enumerate(
@@ -42,7 +42,8 @@
     for row, block, strip in ((0, top, low), (6, bottom, high)):
         for p in range(NP):
             strip[p : p + 1, 0:CC] = block[p, row : row + 1, :]
-            strip[p : p + 1, CC : 2 * CC] = block[p, row + 1 : row + 2, :]
+            second[p : p + 1, 0:CC] = block[p, row + 1 : row + 2, :]
+        strip[0:8, :] = jnp.where(lanes(8) < CC, strip[0:8, :], pltpu.roll(second[...], CC, 1))
         for x in range(2):
             strip[8 + x : 9 + x, :] = marks[x, 15 * (row // 6) : 15 * (row // 6) + 1, :].astype(F32)
         strip[10:16, :] = jnp.zeros((6, 128), F32)
@@ -156,7 +157,7 @@
         marks_m = [lm[x, here, :] for x in range(2)]
         marks_e = [le[x, here, :] for x in range(2)]
         for p in range(NP):
-            m, e = ms[p], es[p]
+            m, e = fm[p, here, :], fe[p, here, :]
             west = jnp.where(first_lane, e, pltpu.roll(m, 1, 1))
             east = jnp.where(last_lane, e, pltpu.roll(m, 127, 1))
             lap = (fm[p, above, :] + fm[p, below, :]) + (west + east)
@@ -220,6 +221,7 @@
             pltpu.SMEM((NP,), F32),
             tile(MROWS),
             tile(MROWS),
+            tile(8),
             pltpu.SemaphoreType.DMA((5,)),
         ],
         compiler_params=pltpu.CompilerParams(vmem_limit_bytes=8 << 20),

time: 25.9 us -> 25.9 us (level)
  no operation moved by 1% of the time
where the time goes in v5:
time: 25.9 us; the launch traced here: 25.7 us
  blocking collectives  15 us (58%)
  starting transfers between devices  7.69 us (30%)
  Pallas kernels  2.93 us (11%)
    all_gather x2, blocking collectives, paired(): lax.all_gather(cells, axis, axis_index_groups=[[i, (i + 1) % count] for i...  15 us
    ppermute x3, starting transfers between devices, exchanged(): return lax.ppermute(cells, ('gy', 'gz'), flat + [(b, a) for a, b in flat])  7.69 us
    pallas_call x1, Pallas kernels, shards(): pl.pallas_call(relax_kernel, out_shape=jax.ShapeDtypeStruct((NP, 2, FR, F...  1.71 us
    pallas_call x1, Pallas kernels, shards(): pl.pallas_call(strips_kernel, out_shape=(tile(MROWS), tile(MROWS), tile(8...  0.97 us
  transfers between devices with their start and end apart: 3, of which 0 were waited for; matrix products, arithmetic and copies ran while one was open for 0% of the time, Pallas kernels for 1%

profile of v5, /device:TPU:1, one launch (start us, length us, event | category | flops | bytes accessed | tf_op | source)
XLA Modules:
  0.0 25.7 jit_solution(18031730171889146510)
XLA Ops:
  0.0 0.0 copy-start
  0.0 0.0 copy-start.1
  0.0 1.0 %strips.1 = (f32[16,128]{1,0:T(8,128)S(1)}, f32[16,128]{1,0:T(8,128)S(1)}, f32[8,128]{1,0:T(8,128)S(1)}) custom-call(f32[8,32,64]{2,1,0:T(8,128)} %bitcast.3, s32[2,64,128]{2,1,0:T(8,128)} %labels.3, f32[8]{0:T(128)} %mobility_hbm.1), custom_call_target="tpu_custom_call" | custom-call | flops 20000 | bytes 200000 | tf_op jit(solution)/shard_map/strips/pallas_call | solution.py:212
  1.0 4.6 %collective-permute-start = (f32[16,128]{1,0:T(8,128)S(1)}, f32[16,128]{1,0:T(8,128)S(1)}, u32[]{:S(2)}, u32[]{:S(2)}) collective-permute-start(f32[16,128]{1,0:T(8,128)S(1)} %get-tuple-element.13), channel_id=1, source_target_pairs={{16,32},{17,33},{18,34},{19,35},{20,36},{21,37},{22,38},{23,39},{2... | collective-permute-start | bytes 24584 | tf_op jit(solution)/shard_map/ppermute | solution.py:199
  5.6 0.0 copy-done
  5.6 0.0 copy-done.1
  5.6 0.2 columns.1
  5.8 5.7 %all-gather = f32[32,128]{1,0:T(8,128)S(1)} all-gather(f32[16,128]{1,0:T(8,128)S(1)} %get-tuple-element.12), channel_id=2, replica_groups={{0,16},{32,48},{64,80},{96,112},{128,144},{160,176},{192,208},{224,240}..., dimensions={0}, use_global_device_ids=true | all-gather | bytes 24576 | tf_op jit(solution)/shard_map/all_gather | solution.py:204
  11.5 0.0 collective-permute-done.yb
  11.5 0.1 sides.1
  11.6 2.4 %collective-permute-start.1 = (f32[16,128]{1,0:T(8,128)S(1)}, f32[16,128]{1,0:T(8,128)S(1)}, u32[]{:S(2)}, u32[]{:S(2)}) collective-permute-start(f32[16,128]{1,0:T(8,128)S(1)} %sides.1), channel_id=1, source_target_pairs={{0,1},{2,3},{4,5},{6,7},{8,9},{10,11},{12,13},{14,15},{16,17},{18,... | collective-permute-start | bytes 24584 | tf_op jit(solution)/shard_map/ppermute | solution.py:199
  14.0 9.3 %all-gather.1 = f32[32,128]{1,0:T(8,128)S(1)} all-gather(f32[16,128]{1,0:T(8,128)S(1)} %sides.1), channel_id=3, replica_groups={{1,2},{3,4},{5,6},{7,8},{9,10},{11,12},{13,14},{15,0},{17,18},{19,20},{..., dimensions={0}, use_global_device_ids=true | all-gather | bytes 24576 | tf_op jit(solution)/shard_map/all_gather | solution.py:204
  23.3 0.0 collective-permute-done.1.za0
  23.3 0.7 %collective-permute-start.2 = (f32[16,128]{1,0:T(8,128)S(1)}, f32[16,128]{1,0:T(8,128)S(1)}, u32[]{:S(2)}, u32[]{:S(2)}) collective-permute-start(f32[16,128]{1,0:T(8,128)S(1)} %sides.1), channel_id=1, source_target_pairs={{30,31},{46,47},{62,63},{78,79},{94,95},{110,111},{126,127},{142,1... | collective-permute-start | bytes 24584 | tf_op jit(solution)/shard_map/ppermute | solution.py:199
  24.0 0.0 collective-permute-done.2.za1
  24.0 1.7 %relax.1 = f32[8,2,64,128]{3,2,1,0:T(8,128)} custom-call(f32[8,128]{1,0:T(8,128)S(1)} %get-tuple-element.11.rates, f32[8,32,64]{2,1,0:T(8,128)S(1)} %bitcast.5, s32[2,64,128]{2,1,0:T(8,128)S(1)} %copy-done.1, f32[2,16,128]{2,1,0:T(8,128)S(1)} %bitcast.7, f32[16,128]{1,0:T(8,128)S(1)} %collective-permute-done.yb, f32[16,128]{1,0:T(8,128)S(1)} %collective-permute-done.1.za0, ...), custom_call_target="tpu_custom_call" | custom-call | flops 8000000 | bytes 900000 | tf_op jit(solution)/shard_map/relax/pallas_call | solution.py:258
Async XLA Ops:
  0.0 5.6 %copy-start = (f32[8,1,32,64]{3,2,1,0:T(8,128)S(1)}, f32[8,1,32,64]{3,2,1,0:T(8,128)}, u32[]{:S(2)}) copy-start(f32[8,1,32,64]{3,2,1,0:T(8,128)} %param.3) | copy-start | bytes 196612
  0.0 5.6 %copy-start.1 = (s32[2,64,128]{2,1,0:T(8,128)S(1)}, s32[2,64,128]{2,1,0:T(8,128)}, u32[]{:S(2)}) copy-start(s32[2,64,128]{2,1,0:T(8,128)} %labels.3) | copy-start | bytes 196612
  1.0 10.5 %collective-permute-start = (f32[16,128]{1,0:T(8,128)S(1)}, f32[16,128]{1,0:T(8,128)S(1)}, u32[]{:S(2)}, u32[]{:S(2)}) collective-permute-start(f32[16,128]{1,0:T(8,128)S(1)} %get-tuple-element.13), channel_id=1, source_target_pairs={{16,32},{17,33},{18,34},{19,35},{20,36},{21,37},{22,38},{23,39},{2... | collective-permute-start | bytes 24584 | tf_op jit(solution)/shard_map/ppermute | solution.py:199
  11.6 11.8 %collective-permute-start.1 = (f32[16,128]{1,0:T(8,128)S(1)}, f32[16,128]{1,0:T(8,128)S(1)}, u32[]{:S(2)}, u32[]{:S(2)}) collective-permute-start(f32[16,128]{1,0:T(8,128)S(1)} %sides.1), channel_id=1, source_target_pairs={{0,1},{2,3},{4,5},{6,7},{8,9},{10,11},{12,13},{14,15},{16,17},{18,... | collective-permute-start | bytes 24584 | tf_op jit(solution)/shard_map/ppermute | solution.py:199
  23.3 0.7 %collective-permute-start.2 = (f32[16,128]{1,0:T(8,128)S(1)}, f32[16,128]{1,0:T(8,128)S(1)}, u32[]{:S(2)}, u32[]{:S(2)}) collective-permute-start(f32[16,128]{1,0:T(8,128)S(1)} %sides.1), channel_id=1, source_target_pairs={{30,31},{46,47},{62,63},{78,79},{94,95},{110,111},{126,127},{142,1... | collective-permute-start | bytes 24584 | tf_op jit(solution)/shard_map/ppermute | solution.py:199
